TPU v7x, 128 devices: a whole 4x4x4 slice. The times are simulated.
128 devices in a mesh: band: 32 (over y, z, core), sub: 4 (over x).
Axes of the slice: x: 4, y: 4, z: 4, core: 2. Of those that a mesh axis runs over, the one named last changes fastest.
Arguments:
- vorticity: float32 [8192, 8192], P(('band', 'sub')), may hold values from -6 to 6
Outputs:
- section_field: float32 [8192, 8192], P(('band', 'sub'))
- coarse_one: float32 [4096, 4096], P('band')
- coarse_two: float32 [2048, 2048], P('band')
All inputs are finite; a program needn't handle non-finite values.
Results may differ from a plain program's by a relative error of at most 0.0001.
Values sent between devices are 32-bit elements; how exact they have to be, the bound alone decides.
A program may use at most 192 MiB of HBM per device.

v0:
```python
import math

import jax
import jax.numpy as jnp
from jax import lax
from jax.sharding import PartitionSpec as P

time_step = 0.2
viscosity = 0.4
forcing = 1.0
force_waves = 4.0
radix = 128


def phase_grid(left_index, right_index, period):
    turn_angle = (left_index * right_index % period).astype(jnp.float32) * (2.0 * math.pi / period)
    return (jnp.cos(turn_angle), jnp.sin(turn_angle))


def phase_table(first_len, second_len, period):
    left_index = lax.broadcasted_iota(jnp.int32, (first_len, 1), 0)
    right_index = lax.broadcasted_iota(jnp.int32, (1, second_len), 1)
    return phase_grid(left_index, right_index, period)


def group_list(first_count, second_count, other_len):
    first_part = lax.iota(jnp.int32, first_count)
    if second_count == 0:
        return first_part
    return jnp.concatenate(
        [first_part, other_len - second_count + lax.iota(jnp.int32, second_count)]
    )


def contract(einsum_form, left_operand, right_operand):
    return jnp.einsum(
        einsum_form,
        left_operand,
        right_operand,
        precision=lax.Precision.HIGHEST,
        preferred_element_type=jnp.float32,
    )


def forward_modes(real_part, imag_part, group_index, leading):
    batch_size, length = real_part.shape
    other_len = length // radix
    mode_count = group_index.shape[0] * radix
    real_cube = real_part.reshape(batch_size, radix, other_len)
    cos_outer, sin_outer = phase_table(radix, radix, radix)
    first_real = contract("bpq,pk->bkq", real_cube, cos_outer)
    first_imag = -contract("bpq,pk->bkq", real_cube, sin_outer)
    if imag_part is not None:
        imag_cube = imag_part.reshape(batch_size, radix, other_len)
        first_real = first_real + contract("bpq,pk->bkq", imag_cube, sin_outer)
        first_imag = first_imag + contract("bpq,pk->bkq", imag_cube, cos_outer)
    twist_cos, twist_sin = phase_table(radix, other_len, length)
    second_real = first_real * twist_cos + first_imag * twist_sin
    second_imag = first_imag * twist_cos - first_real * twist_sin
    cos_inner, sin_inner = phase_grid(
        lax.broadcasted_iota(jnp.int32, (other_len, 1), 0), group_index[None, :], other_len
    )
    einsum_form = "bkq,qj->jkb" if leading else "bkq,qj->bjk"
    out_shape = (mode_count, batch_size) if leading else (batch_size, mode_count)
    out_real = contract(einsum_form, second_real, cos_inner) + contract(
        einsum_form, second_imag, sin_inner
    )
    out_imag = contract(einsum_form, second_imag, cos_inner) - contract(
        einsum_form, second_real, sin_inner
    )
    return (out_real.reshape(out_shape), out_imag.reshape(out_shape))


def backward_modes(real_part, imag_part, length, leading, real_only, group_index):
    batch_size, mode_count = real_part.shape
    other_len = length // radix
    groups = mode_count // radix
    real_cube = real_part.reshape(batch_size, groups, radix)
    imag_cube = imag_part.reshape(batch_size, groups, radix)
    cos_inner, sin_inner = phase_grid(
        group_index[:, None], lax.broadcasted_iota(jnp.int32, (1, other_len), 1), other_len
    )
    first_real = contract("bjk,jq->bkq", real_cube, cos_inner) - contract(
        "bjk,jq->bkq", imag_cube, sin_inner
    )
    first_imag = contract("bjk,jq->bkq", real_cube, sin_inner) + contract(
        "bjk,jq->bkq", imag_cube, cos_inner
    )
    twist_cos, twist_sin = phase_table(radix, other_len, length)
    second_real = first_real * twist_cos - first_imag * twist_sin
    second_imag = first_real * twist_sin + first_imag * twist_cos
    cos_outer, sin_outer = phase_table(radix, radix, radix)
    einsum_form = "bkq,kp->pqb" if leading else "bkq,kp->bpq"
    out_shape = (length, batch_size) if leading else (batch_size, length)
    out_real = (
        contract(einsum_form, second_real, cos_outer)
        - contract(einsum_form, second_imag, sin_outer)
    ).reshape(out_shape)
    if real_only:
        return out_real
    out_imag = (
        contract(einsum_form, second_real, sin_outer)
        + contract(einsum_form, second_imag, cos_outer)
    ).reshape(out_shape)
    return (out_real, out_imag)


def local(vorticity):
    row_count, length = vorticity.shape
    devices = lax.axis_size(("band", "sub"))
    place_index = lax.axis_index(("band", "sub"))
    other_len = length // radix
    cutoff = length // 3
    wave_groups = cutoff // radix + 1
    kept_width = wave_groups * radix
    slab_width = kept_width // devices
    column_groups = group_list(kept_width // radix, 0, other_len)
    row_groups = group_list(wave_groups, wave_groups, other_len)
    kept_rows = 2 * wave_groups * radix
    col_real, col_imag = forward_modes(vorticity, None, column_groups, True)
    col_real, col_imag = (
        lax.all_to_all(col_real, ("band", "sub"), split_axis=0, concat_axis=1, tiled=True),
        lax.all_to_all(col_imag, ("band", "sub"), split_axis=0, concat_axis=1, tiled=True),
    )
    vort_real, vort_imag = forward_modes(col_real, col_imag, row_groups, False)
    wave_x = place_index * slab_width + lax.broadcasted_iota(jnp.int32, (slab_width, 1), 0)
    index_y = lax.broadcasted_iota(jnp.int32, (1, kept_rows), 1)
    wave_y = jnp.where(index_y < wave_groups * radix, index_y, index_y - kept_rows)
    kept_modes = ((wave_x <= cutoff) & (jnp.abs(wave_y) <= cutoff)).astype(jnp.float32)
    factor = 2.0 * math.pi / length
    kappa_x = factor * wave_x.astype(jnp.float32)
    kappa_y = factor * wave_y.astype(jnp.float32)
    kappa_sq = kappa_x * kappa_x + kappa_y * kappa_y
    inverse_sq = jnp.where(kappa_sq > 0, 1.0 / jnp.where(kappa_sq > 0, kappa_sq, 1.0), 0.0)
    vort_real = vort_real * kept_modes
    vort_imag = vort_imag * kept_modes
    stream_real = vort_real * inverse_sq
    stream_imag = vort_imag * inverse_sq
    weight = jnp.where(wave_x == 0, 1.0, 2.0) / (float(length) * float(length))
    field_real = (
        jnp.stack(
            [
                -kappa_y * stream_imag,
                kappa_x * stream_imag,
                -kappa_x * vort_imag,
                -kappa_y * vort_imag,
            ]
        )
        * weight
    )
    field_imag = (
        jnp.stack(
            [
                kappa_y * stream_real,
                -kappa_x * stream_real,
                kappa_x * vort_real,
                kappa_y * vort_real,
            ]
        )
        * weight
    )
    grid_real, grid_imag = backward_modes(
        field_real.reshape(4 * slab_width, kept_rows),
        field_imag.reshape(4 * slab_width, kept_rows),
        length,
        True,
        False,
        row_groups,
    )
    grid_real = grid_real.reshape(length, 4, slab_width)
    grid_imag = grid_imag.reshape(length, 4, slab_width)
    grid_real, grid_imag = (
        lax.all_to_all(grid_real, ("band", "sub"), split_axis=0, concat_axis=2, tiled=True),
        lax.all_to_all(grid_imag, ("band", "sub"), split_axis=0, concat_axis=2, tiled=True),
    )
    physical = backward_modes(
        grid_real.reshape(row_count * 4, kept_width),
        grid_imag.reshape(row_count * 4, kept_width),
        length,
        False,
        True,
        column_groups,
    )
    physical = physical.reshape(row_count, 4, length)
    positions = (
        place_index * row_count + lax.broadcasted_iota(jnp.int32, (row_count, 1), 0)
    ).astype(jnp.float32)
    drive_term = forcing * jnp.sin(2.0 * math.pi * force_waves / length * positions)
    advect = physical[:, 0] * physical[:, 2] + physical[:, 1] * physical[:, 3] - drive_term
    adv_real, adv_imag = forward_modes(advect, None, column_groups, True)
    adv_real, adv_imag = (
        lax.all_to_all(adv_real, ("band", "sub"), split_axis=0, concat_axis=1, tiled=True),
        lax.all_to_all(adv_imag, ("band", "sub"), split_axis=0, concat_axis=1, tiled=True),
    )
    adv_real, adv_imag = forward_modes(adv_real, adv_imag, row_groups, False)
    adv_real = adv_real * kept_modes
    adv_imag = adv_imag * kept_modes
    half_step = 0.5 * time_step
    next_real = (vort_real + half_step * (-adv_real - viscosity * kappa_sq * vort_real)) * weight
    next_imag = (vort_imag + half_step * (-adv_imag - viscosity * kappa_sq * vort_imag)) * weight
    pieces = [backward_modes(next_real, next_imag, length, True, False, row_groups)]
    for divisor in (2, 4):
        grid_size = length // divisor
        upper_half = grid_size // 2
        zero_column = jnp.zeros((slab_width, 1), jnp.float32)
        block_real = jnp.concatenate(
            [next_real[:, :upper_half], zero_column, next_real[:, kept_rows - upper_half + 1 :]],
            axis=1,
        )
        block_imag = jnp.concatenate(
            [next_imag[:, :upper_half], zero_column, next_imag[:, kept_rows - upper_half + 1 :]],
            axis=1,
        )
        pieces.append(
            backward_modes(
                block_real,
                block_imag,
                grid_size,
                True,
                False,
                group_list(grid_size // radix, 0, grid_size // radix),
            )
        )
    arrived = [
        (
            lax.all_to_all(pieces[0][0], ("band", "sub"), split_axis=0, concat_axis=1, tiled=True),
            lax.all_to_all(pieces[0][1], ("band", "sub"), split_axis=0, concat_axis=1, tiled=True),
        )
    ]
    for entry_pair in pieces[1:]:
        arrived.append(
            (
                lax.all_to_all(
                    entry_pair[0], ("band", "sub"), split_axis=0, concat_axis=1, tiled=True
                ),
                lax.all_to_all(
                    entry_pair[1], ("band", "sub"), split_axis=0, concat_axis=1, tiled=True
                ),
            )
        )
    section_field = backward_modes(arrived[0][0], arrived[0][1], length, False, True, column_groups)
    coarse_list = []
    for divisor, entry_pair in zip((2, 4), arrived[1:]):
        grid_size = length // divisor
        upper_half = grid_size // 2
        coarse_list.append(
            backward_modes(
                entry_pair[0][:, :upper_half],
                entry_pair[1][:, :upper_half],
                grid_size,
                False,
                True,
                group_list(upper_half // radix, 0, grid_size // radix),
            )
        )
    coarse_one, coarse_two = (
        lax.all_gather(coarse_list[0], "sub", axis=0, tiled=True),
        lax.all_gather(coarse_list[1], "sub", axis=0, tiled=True),
    )
    return (section_field, coarse_one, coarse_two)


def solution(mesh):
    return jax.shard_map(
        local,
        mesh=mesh,
        in_specs=(P(("band", "sub"), None),),
        out_specs=(P(("band", "sub"), None), P("band", None), P("band", None)),
        check_vma=False,
    )
```

profile of v0, /device:TPU:0, one launch (start us, length us, event | category | flops | bytes accessed | tf_op | source)
XLA Modules:
  0.0 805.3 jit_solution(16551188571696253166)
XLA Ops:
  33.8 11.8 %all-to-all-start.1 = ((f32[128,1,1408]{2,1,0:T(1,128)}), f32[128,1,1408]{2,1,0:T(1,128)}, u32[]{:S(2)}, u32[]{:S(2)}) async-start(f32[128,1,1408]{2,1,0:T(1,128)} %reshape.1213), calls=%async_computation.1 | async-start | bytes 1441792 | tf_op jit(solution)/shard_map/all_to_all | solution.py:123
  55.3 5.4 all-to-all-done.1
  74.1 6.6 all-to-all-done
  111.3 4.7 fusion.44
  116.1 5.1 multiply_subtract_fusion.1
  121.2 4.7 fusion.6
  125.9 6.6 add_bitcast_fusion
  132.5 4.9 copy.171
  137.4 12.8 %reshape.1207 = f32[8192,4,22]{2,1,0:T(4,128)} reshape(f32[128,64,88]{2,1,0:T(8,128)} %copy.171) | data formatting | bytes 5767168 | tf_op jit(solution)/shard_map/reshape;reshape | solution.py:171
  150.3 22.7 %reshape.1217 = f32[128,1,5632]{2,1,0:T(1,128)} reshape(f32[8192,4,22]{2,1,0:T(4,128)} %reshape.1207) | data formatting | bytes 5767168
  173.0 6.1 all-to-all-start.3
  179.1 6.5 fusion.8
  185.6 6.4 subtract_bitcast_fusion.1
  192.0 4.8 copy.168
  196.9 12.9 %reshape.1206 = f32[8192,4,22]{2,1,0:T(4,128)} reshape(f32[128,64,88]{2,1,0:T(8,128)} %copy.168) | data formatting | bytes 5767168 | tf_op jit(solution)/shard_map/reshape;reshape | solution.py:170
  209.8 22.9 %reshape.1215 = f32[128,1,5632]{2,1,0:T(1,128)} reshape(f32[8192,4,22]{2,1,0:T(4,128)} %reshape.1206) | data formatting | bytes 5767168
  232.6 10.3 %all-to-all-start.2 = ((f32[128,1,5632]{2,1,0:T(1,128)}), f32[128,1,5632]{2,1,0:T(1,128)}, u32[]{:S(2)}, u32[]{:S(2)}) async-start(f32[128,1,5632]{2,1,0:T(1,128)} %reshape.1215), calls=%async_computation.2 | async-start | bytes 5767168 | tf_op jit(solution)/shard_map/all_to_all | solution.py:173
  243.7 9.3 %reduce.4 = f32[128,5632]{1,0:T(8,128)S(1)} reduce(f32[128,1,5632]{2,1,0:T(1,128)} %all-to-all-done.3, f32[]{:T(128)} %broadcast.1746), dimensions={1}, to_apply=%all_to_all.147.reduce_sub_computation | reduce | bytes 5767172 | tf_op jit(solution)/shard_map/all_to_all | solution.py:174
  253.1 25.4 %reshape.1218 = f32[8192,4,22]{2,1,0:T(4,128)} reshape(f32[128,5632]{1,0:T(8,128)S(1)} %reduce.4) | data formatting | bytes 5767168
  278.4 17.9 %copy.221 = f32[128,64,4,22]{3,0,2,1:T(8,128)} copy(f32[128,64,4,22]{3,2,1,0:T(4,128)} %bitcast.470) | data formatting | bytes 5767168 | tf_op jit(solution)/shard_map/all_to_all | solution.py:174
  296.4 15.5 %reshape_reshape.20 = f32[256,22,128]{2,1,0:T(8,128)S(1)} reshape(f32[64,4,128,22]{3,2,1,0:T(8,128)} %bitcast.471) | data formatting | bytes 5767168 | tf_op jit(solution)/shard_map/reshape;reshape | solution.py:79
  311.9 9.0 %fusion.290 = f32[256,128,64]{1,2,0:T(8,128)} fusion(f32[256,22,128]{2,1,0:T(8,128)S(1)} %reshape_reshape.20), kind=kOutput, calls=%fused_computation.338 | convolution fusion | flops 553667840 | bytes 11272192 | tf_op jit(solution)/shard_map/bjk,jq->bkq/dot_general | solution.py:36
  320.9 9.5 %fusion.295 = f32[256,128,64]{1,2,0:T(8,128)} fusion(f32[256,22,128]{2,1,0:T(8,128)S(1)} %reshape_reshape.20), kind=kOutput, calls=%fused_computation.343 | convolution fusion | flops 553667840 | bytes 11272192 | tf_op jit(solution)/shard_map/bjk,jq->bkq/dot_general | solution.py:36
  330.4 9.3 %reduce.5 = f32[128,5632]{1,0:T(8,128)S(1)} reduce(f32[128,1,5632]{2,1,0:T(1,128)} %all-to-all-done.2, f32[]{:T(128)} %broadcast.1746), dimensions={1}, to_apply=%all_to_all.144.reduce_sub_computation | reduce | bytes 5767172 | tf_op jit(solution)/shard_map/all_to_all | solution.py:173
  339.8 25.6 %reshape.1216 = f32[8192,4,22]{2,1,0:T(4,128)} reshape(f32[128,5632]{1,0:T(8,128)S(1)} %reduce.5) | data formatting | bytes 5767168
  365.3 17.7 %copy.222 = f32[128,64,4,22]{3,0,2,1:T(8,128)} copy(f32[128,64,4,22]{3,2,1,0:T(4,128)} %bitcast.472) | data formatting | bytes 5767168 | tf_op jit(solution)/shard_map/all_to_all | solution.py:173
  383.1 15.5 %reshape_reshape.18 = f32[256,22,128]{2,1,0:T(8,128)S(1)} reshape(f32[64,4,128,22]{3,2,1,0:T(8,128)} %bitcast.473) | data formatting | bytes 5767168 | tf_op jit(solution)/shard_map/reshape;reshape | solution.py:78
  400.3 9.1 %fusion.297 = f32[256,128,64]{1,2,0:T(8,128)} fusion(f32[256,22,128]{2,1,0:T(8,128)S(1)} %reshape_reshape.18), kind=kOutput, calls=%fused_computation.345 | convolution fusion | flops 553667840 | bytes 11272192 | tf_op jit(solution)/shard_map/bjk,jq->bkq/dot_general | solution.py:36
  409.4 17.6 %multiply_subtract_fusion = (f32[256,128,64]{1,2,0:T(8,128)S(1)}, f32[256,128,64]{1,2,0:T(8,128)}) fusion(f32[128,64]{0,1:T(8,128)S(1)} %get-tuple-element.39, f32[128,64]{0,1:T(8,128)S(1)} %get-tuple-element.40, f32[256,128,64]{1,2,0:T(8,128)} %fusion.295, f32[256,128,64]{1,2,0:T(8,128)} %fusion.297, f32[256,128,64]{1,2,0:T(8,128)} %fusion.290, ...), kind=kOutput, calls=%fused_computation.8 | convolution fusion | flops 570445056 | bytes 44892160 | tf_op jit(solution)/shard_map/bjk,jq->bkq/dot_general | solution.py:36
  427.0 16.4 %fusion = f32[128,256,64]{1,0,2:T(8,128)S(1)} fusion(f32[256,128,64]{1,2,0:T(8,128)} %get-tuple-element.4), kind=kOutput, calls=%fused_computation.2 | convolution fusion | flops 3221454848 | bytes 16777216 | tf_op jit(solution)/shard_map/bkq,kp->bpq/dot_general | solution.py:36
  443.5 18.2 %subtract_bitcast_fusion = f32[256,128,64]{0,1,2:T(8,128)} fusion(f32[128,256,64]{1,0,2:T(8,128)S(1)} %fusion, f32[256,128,64]{1,2,0:T(8,128)S(1)} %get-tuple-element.3), kind=kOutput, calls=%fused_computation.6 | convolution fusion | flops 3223552000 | bytes 25165824 | tf_op jit(solution)/shard_map/bkq,kp->bpq/dot_general | solution.py:36
  461.7 16.5 %copy.138 = f32[256,128,64]{2,1,0:T(8,128)} copy(f32[256,128,64]{0,1,2:T(8,128)} %subtract_bitcast_fusion) | data formatting | bytes 16777216 | tf_op jit(solution)/shard_map/sub | solution.py:96
  478.2 15.6 %reshape_reshape.21 = f32[64,4,8192]{2,1,0:T(4,128)} reshape(f32[256,128,64]{2,1,0:T(8,128)} %copy.138) | data formatting | bytes 16777216 | tf_op jit(solution)/shard_map/reshape;reshape | solution.py:184
  493.8 20.4 %fusion.31 = f32[64,8192]{1,0:T(8,128)S(1)} fusion(f32[64,4,8192]{2,1,0:T(4,128)} %reshape_reshape.21), kind=kLoop, calls=%fused_computation.49 | loop fusion | flops 1572864 | bytes 10485760 | tf_op jit(solution)/shard_map/add | solution.py:189
  537.0 10.2 %all-to-all-start.5 = ((f32[128,1,1408]{2,1,0:T(1,128)}), f32[128,1,1408]{2,1,0:T(1,128)}, u32[]{:S(2)}, u32[]{:S(2)}) async-start(f32[128,1,1408]{2,1,0:T(1,128)} %reshape.1221), calls=%async_computation.5 | async-start | bytes 1441792 | tf_op jit(solution)/shard_map/all_to_all | solution.py:193
  562.2 6.0 all-to-all-start.4
  633.9 7.6 all-to-all-start.10
  659.2 9.9 %all-to-all-start.11 = ((f32[128,1,352]{2,1,0:T(1,128)}), f32[128,1,352]{2,1,0:T(1,128)S(1)}, u32[]{:S(2)}, u32[]{:S(2)}) async-start(f32[128,1,352]{2,1,0:T(1,128)} %reshape.1233), calls=%async_computation.11 | async-start | bytes 393216 | tf_op jit(solution)/shard_map/all_to_all | solution.py:236
  672.5 6.5 all-to-all-done.11
  679.0 4.9 all-to-all-start.8
  689.5 6.4 all-to-all-done.8
  695.8 5.7 all-to-all-start.9
  707.2 5.8 all-to-all-done.9
  713.1 5.9 all-to-all-start.7
  727.0 7.0 all-to-all-done.7
  734.0 5.7 all-to-all-start.6
  742.2 16.9 %all_gather.7 = f32[64,2048]{1,0:T(8,128)} all-gather(f32[16,2048]{1,0:T(8,128)S(1)} %reshape.1133), channel_id=1, replica_groups=mesh['band'=32,'sub'=4] {'sub'}, dimensions={0}, use_global_device_ids=true | all-gather | bytes 655360 | tf_op jit(solution)/shard_map/all_gather | solution.py:258
  789.3 4.8 reshape.1119
  (328 shorter events, 261.9 us)
Async XLA Ops:
  15.7 3.8 copy-start.7
  33.8 26.9 %all-to-all-start.1 = ((f32[128,1,1408]{2,1,0:T(1,128)}), f32[128,1,1408]{2,1,0:T(1,128)}, u32[]{:S(2)}, u32[]{:S(2)}) async-start(f32[128,1,1408]{2,1,0:T(1,128)} %reshape.1213), calls=%async_computation.1 | async-start | bytes 1441792 | tf_op jit(solution)/shard_map/all_to_all | solution.py:123
  45.6 3.2 copy-start.1
  55.2 36.6 %copy-start.46 = (pred[22]{0:T(512)(128)(4,1)}, pred[22]{0:T(512)(128)(4,1)S(1)}, u32[]{:S(2)}) copy-start(pred[22]{0:T(512)(128)(4,1)S(1)} %fusion.422) | copy-start | bytes 70
  55.2 36.6 %copy-start.49 = (f32[22]{0:T(128)}, f32[22]{0:T(128)S(1)}, u32[]{:S(2)}) copy-start(f32[22]{0:T(128)S(1)} %get-tuple-element.44) | copy-start | bytes 268
  55.2 36.6 %copy-start.41 = (pred[5632]{0:T(1024)(128)(4,1)}, pred[5632]{0:T(1024)(128)(4,1)S(1)}, u32[]{:S(2)}) copy-start(pred[5632]{0:T(1024)(128)(4,1)S(1)} %abs_compare_fusion) | copy-start | bytes 16900
  60.7 20.0 %all-to-all-start = ((f32[128,1,1408]{2,1,0:T(1,128)}), f32[128,1,1408]{2,1,0:T(1,128)S(1)}, u32[]{:S(2)}, u32[]{:S(2)}) async-start(f32[128,1,1408]{2,1,0:T(1,128)} %reshape.1211), calls=%async_computation | async-start | bytes 1441792 | tf_op jit(solution)/shard_map/all_to_all | solution.py:122
  65.4 50.7 %copy-start.37 = (s32[44]{0:T(128)}, s32[44]{0:T(128)S(1)}, u32[]{:S(2)}) copy-start(s32[44]{0:T(128)S(1)} %pad_add_fusion) | copy-start | bytes 532
  65.4 26.4 %copy-start.33 = (f32[5632]{0:T(1024)}, f32[5632]{0:T(1024)S(1)}, u32[]{:S(2)}) copy-start(f32[5632]{0:T(1024)S(1)} %get-tuple-element.46) | copy-start | bytes 67588
  84.0 2.0 copy-start.15
  84.0 2.0 copy-start.16
  88.6 6.1 copy-start.8
  90.8 3.8 copy-start.11
  102.1 4.2 copy-start.21
  102.1 4.2 copy-start.22
  102.1 4.2 copy-start.23
  111.3 4.8 copy-start.10
  121.2 4.7 copy-start.5
  173.0 59.7 %all-to-all-start.3 = ((f32[128,1,5632]{2,1,0:T(1,128)}), f32[128,1,5632]{2,1,0:T(1,128)}, u32[]{:S(2)}, u32[]{:S(2)}) async-start(f32[128,1,5632]{2,1,0:T(1,128)} %reshape.1217), calls=%async_computation.3 | async-start | bytes 5767168 | tf_op jit(solution)/shard_map/all_to_all | solution.py:174
  232.6 97.8 %all-to-all-start.2 = ((f32[128,1,5632]{2,1,0:T(1,128)}), f32[128,1,5632]{2,1,0:T(1,128)}, u32[]{:S(2)}, u32[]{:S(2)}) async-start(f32[128,1,5632]{2,1,0:T(1,128)} %reshape.1215), calls=%async_computation.2 | async-start | bytes 5767168 | tf_op jit(solution)/shard_map/all_to_all | solution.py:173
  537.0 25.2 %all-to-all-start.5 = ((f32[128,1,1408]{2,1,0:T(1,128)}), f32[128,1,1408]{2,1,0:T(1,128)}, u32[]{:S(2)}, u32[]{:S(2)}) async-start(f32[128,1,1408]{2,1,0:T(1,128)} %reshape.1221), calls=%async_computation.5 | async-start | bytes 1441792 | tf_op jit(solution)/shard_map/all_to_all | solution.py:193
  547.2 3.2 copy-start.3
  556.7 11.6 %copy-start.9 = (f32[22,44,128]{2,1,0:T(8,128)S(1)}, f32[22,44,128]{2,1,0:T(8,128)}, u32[]{:S(2)}) copy-start(f32[22,44,128]{2,1,0:T(8,128)} %copy-done.8) | copy-start | bytes 1486852
  556.7 11.7 %copy-start.12 = (f32[22,44,128]{2,1,0:T(8,128)S(1)}, f32[22,44,128]{2,1,0:T(8,128)}, u32[]{:S(2)}) copy-start(f32[22,44,128]{2,1,0:T(8,128)} %copy-done.11) | copy-start | bytes 1486852
  562.2 21.4 %all-to-all-start.4 = ((f32[128,1,1408]{2,1,0:T(1,128)}), f32[128,1,1408]{2,1,0:T(1,128)S(1)}, u32[]{:S(2)}, u32[]{:S(2)}) async-start(f32[128,1,1408]{2,1,0:T(1,128)} %reshape.1219), calls=%async_computation.4 | async-start | bytes 1441792 | tf_op jit(solution)/shard_map/all_to_all | solution.py:192
  568.4 42.7 %copy-start.35 = (f32[128,32]{0,1:T(8,128)}, f32[128,32]{0,1:T(8,128)S(1)}, u32[]{:S(2)}) copy-start(f32[128,32]{0,1:T(8,128)S(1)} %get-tuple-element.48) | copy-start | bytes 49156
  596.5 5.4 copy-start.39
  614.9 4.8 copy-start.45
  614.9 4.8 copy-start.48
  614.9 4.8 copy-start.51
  624.1 4.7 copy-start.32
  628.7 2.6 copy-start.31
  629.8 11.6 %copy-start.29 = (f32[128,704]{0,1:S(1)}, f32[128,704]{0,1}, u32[]{:S(2)}) copy-start(f32[128,704]{0,1} %fusion.201) | copy-start | bytes 1081348
  629.9 11.6 %copy-start.30 = (f32[128,704]{0,1:S(1)}, f32[128,704]{0,1}, u32[]{:S(2)}) copy-start(f32[128,704]{0,1} %fusion.170) | copy-start | bytes 1081348
  633.9 25.3 %all-to-all-start.10 = ((f32[128,1,352]{2,1,0:T(1,128)}), f32[128,1,352]{2,1,0:T(1,128)S(1)}, u32[]{:S(2)}, u32[]{:S(2)}) async-start(f32[128,1,352]{2,1,0:T(1,128)} %reshape.1231), calls=%async_computation.10 | async-start | bytes 393216 | tf_op jit(solution)/shard_map/all_to_all | solution.py:233
  642.3 3.1 copy-start.27
  642.3 3.1 copy-start.28
  646.2 3.1 copy-start.14
  651.4 3.5 copy-start.13
  659.2 19.8 %all-to-all-start.11 = ((f32[128,1,352]{2,1,0:T(1,128)}), f32[128,1,352]{2,1,0:T(1,128)S(1)}, u32[]{:S(2)}, u32[]{:S(2)}) async-start(f32[128,1,352]{2,1,0:T(1,128)} %reshape.1233), calls=%async_computation.11 | async-start | bytes 393216 | tf_op jit(solution)/shard_map/all_to_all | solution.py:236
  679.0 16.8 %all-to-all-start.8 = ((f32[128,1,704]{2,1,0:T(1,128)}), f32[128,1,704]{2,1,0:T(1,128)S(1)}, u32[]{:S(2)}, u32[]{:S(2)}) async-start(f32[128,1,704]{2,1,0:T(1,128)} %reshape.1227), calls=%async_computation.8 | async-start | bytes 786432 | tf_op jit(solution)/shard_map/all_to_all | solution.py:233
  695.8 17.2 %all-to-all-start.9 = ((f32[128,1,704]{2,1,0:T(1,128)}), f32[128,1,704]{2,1,0:T(1,128)}, u32[]{:S(2)}, u32[]{:S(2)}) async-start(f32[128,1,704]{2,1,0:T(1,128)} %reshape.1229), calls=%async_computation.9 | async-start | bytes 786432 | tf_op jit(solution)/shard_map/all_to_all | solution.py:236
  713.1 20.9 %all-to-all-start.7 = ((f32[128,1,1408]{2,1,0:T(1,128)}), f32[128,1,1408]{2,1,0:T(1,128)}, u32[]{:S(2)}, u32[]{:S(2)}) async-start(f32[128,1,1408]{2,1,0:T(1,128)} %reshape.1225), calls=%async_computation.7 | async-start | bytes 1441792 | tf_op jit(solution)/shard_map/all_to_all | solution.py:227
  722.3 2.2 copy-start.36
  722.4 2.1 copy-start.25
  734.0 32.3 %all-to-all-start.6 = ((f32[128,1,1408]{2,1,0:T(1,128)}), f32[128,1,1408]{2,1,0:T(1,128)}, u32[]{:S(2)}, u32[]{:S(2)}) async-start(f32[128,1,1408]{2,1,0:T(1,128)} %reshape.1223), calls=%async_computation.6 | async-start | bytes 1441792 | tf_op jit(solution)/shard_map/all_to_all | solution.py:226
  739.7 54.4 %all-gather.2.cloned.1.call-start = ((), (), s32[]{:S(2)}) async-start(), calls=%async_computation.12 | async-start | bytes 2621440 | tf_op jit(solution)/shard_map/all_gather | solution.py:257
  794.1 3.2 copy-start.24
  (17 other events, 21.9 us)
Sparse Core Ops, SparseCore 0:
  742.8 32.3 all-gather.1
where the time goes:
time: 817 us; the launch traced here: 805 us
  local copies, waits for them, and re-layouts  343 us (42%)
  matrix products  219 us (27%)
  starting transfers between devices  88.7 us (11%)
  other arithmetic  77.7 us (10%)
  waiting for transfers between devices  44.1 us (5%)
  blocking collectives  16.9 us (2%)
  between operations  16.2 us (2%)
    dot_general x58, matrix products, contract(): jnp.einsum(einsum_form, left_operand, right_operand, precision=lax.Precis...  179 us
    unnamed x146, local copies, waits for them, and re-layouts  134 us
    unnamed x26, matrix products  40.6 us
    sub x7, local copies, waits for them, and re-layouts, backward_modes(): contract(einsum_form, second_real, cos_outer)  23.9 us
    add x1, other arithmetic, local(): physical[:, 0] * physical[:, 2] + physical[:, 1] * physical[:, 3]  20.4 us
    all_to_all x1, local copies, waits for them, and re-layouts, local(): lax.all_to_all(grid_imag, ('band', 'sub'), split_axis=0, concat_axis=2, t...  17.9 us
    all_to_all x1, local copies, waits for them, and re-layouts, local(): lax.all_to_all(grid_real, ('band', 'sub'), split_axis=0, concat_axis=2, t...  17.7 us
    another operation x2, local copies, waits for them, and re-layouts, local(): grid_imag = grid_imag.reshape(length, 4, slab_width)  17.7 us
  transfers between devices with their start and end apart: 13, of which 8 were waited for; matrix products, arithmetic and copies ran while one was open for 32% of the time, Pallas kernels for 0%

commit v1 on v0

v1 whole, which is shorter than its diff:
```python
import functools
import math

import jax
import jax.numpy as jnp
import ml_dtypes
import numpy as np
from jax import lax
from jax.experimental import pallas as pl
from jax.experimental.pallas import tpu as pltpu
from jax.sharding import PartitionSpec as P

time_step = 0.2
viscosity = 0.4
forcing = 1.0
force_waves = 4.0

N = 8192
CUT = N // 3
DEV = 128
AXES = ("band", "sub")
f32 = jnp.float32
bf16 = jnp.bfloat16


def halves(table):
    table = np.asarray(table, np.float64).astype(np.float32)
    high = table.astype(ml_dtypes.bfloat16)
    low = (table - high.astype(np.float32)).astype(ml_dtypes.bfloat16)
    return np.stack([high, low])


def wave_of(t):
    return np.where(t % 2 == 1, -(t + 1) // 2, t // 2)


def slot_index():
    e, i = np.meshgrid(np.arange(16), np.arange(11), indexing="ij")
    return e + 16 * i


def forward_row_tables():
    t = slot_index()
    p = np.arange(256)
    out = np.zeros((2, 16, 2, 12, 2, 256))
    ang = 2 * np.pi * ((wave_of(t)[:, :, None] * p) % 256) / 256
    out[0, :, 0, :11, 0], out[0, :, 0, :11, 1] = np.cos(ang), np.sin(ang)
    out[0, :, 1, :11, 0], out[0, :, 1, :11, 1] = -np.sin(ang), np.cos(ang)
    ang = 2 * np.pi * ((16 * t[:, :, None] * p) % N) / N
    odd = (t % 2 == 1)[:, :, None]
    out[1, :, 0, :11, 0], out[1, :, 1, :11, 0] = np.where(odd, 0, np.cos(ang)), np.where(odd, 0, -np.sin(ang))
    out[1, :, 0, :11, 1], out[1, :, 1, :11, 1] = np.where(odd, np.cos(ang), 0), np.where(odd, -np.sin(ang), 0)
    out *= (t <= 170)[None, :, None, :, None, None] if False else 1.0
    return halves(out[0].reshape(384, 512)), halves(out[1].reshape(384, 512))


def backward_row_values(t, length):
    plen = length // 32
    p = np.arange(plen)
    ang = 2 * np.pi * ((wave_of(t)[..., None] * p) % plen) / plen
    gen = np.zeros(t.shape + (2, 2, plen))
    gen[..., 0, 0, :], gen[..., 1, 0, :] = np.cos(ang), -np.sin(ang)
    gen[..., 0, 1, :], gen[..., 1, 1, :] = np.sin(ang), np.cos(ang)
    ang = 2 * np.pi * ((16 * t[..., None] * p) % length) / length
    odd = (t % 2 == 1)[..., None]
    spe = np.zeros(t.shape + (2, 2, plen))
    spe[..., 0, 0, :], spe[..., 1, 0, :] = np.where(odd, 0, np.cos(ang)), np.where(odd, 0, -np.sin(ang))
    spe[..., 0, 1, :], spe[..., 1, 1, :] = np.where(odd, np.cos(ang), 0), np.where(odd, -np.sin(ang), 0)
    return np.stack([gen, spe]).reshape((2,) + t.shape + (2, 2 * plen))


def backward_field_tables():
    v = backward_row_values(slot_index(), N)
    v = np.moveaxis(v, 3, 1).reshape(2, 352, 512)
    return halves(v[0]), halves(v[1])


def backward_next_tables():
    t = slot_index()
    v = backward_row_values(t, N)
    full = np.zeros((2, 16, 32, 512))
    for ri in range(2):
        full[:, :, ri * 11 : ri * 11 + 11] = v[:, :, :, ri]
    v1 = backward_row_values(t, N // 2)
    one = np.zeros((2, 2, 16, 32, 256))
    for ii in range(4):
        for ri in range(2):
            for ipar in range(2):
                one[:, ipar, :, 22 + 2 * ii + ri] = v1[:, :, 2 * ii + ipar, ri]
    v2 = backward_row_values(t, N // 4)
    two = np.zeros((2, 4, 16, 32, 128))
    for i in range(4):
        for ri in range(2):
            two[:, i, :, 30 + ri] = v2[:, :, i, ri]
    return (
        halves(full.reshape(2, 512, 512)),
        halves(one.reshape(2, 2, 512, 256)),
        halves(two.reshape(2, 4, 512, 128)),
    )


def row_twiddle(length):
    plen = length // 32
    ang = 2 * np.pi * np.arange(16)[:, None] * np.arange(plen) / length
    return (0.5 * np.stack([np.cos(ang), np.sin(ang)])).astype(np.float32)


def column_outer():
    ang = 2 * np.pi * ((np.arange(128)[:, None] * np.arange(128)) % 128) / 128
    c, s = np.cos(ang), np.sin(ang)
    return halves(np.block([[c, s], [-s, c]])), halves(np.block([[c, -s], [s, c]]))


def column_twiddle(rows_each, copies):
    length = DEV * rows_each
    ang = 2 * np.pi * np.arange(128)[:, None] * np.arange(rows_each) / length
    return np.stack([np.tile(np.cos(ang), (1, copies)), np.tile(np.sin(ang), (1, copies))]).astype(np.float32)


def column_inner(rows_each, copies, sign):
    j = np.arange(64)
    signed = np.where(j < 32, j, j - 64)
    ang = 2 * np.pi * ((signed[:, None] * np.arange(rows_each)) % rows_each) / rows_each
    keep = ((signed >= -rows_each // 2) & (signed < rows_each // 2))[:, None]
    c, s = np.cos(ang) * keep, np.sin(ang) * keep
    out = np.zeros((copies, 2, 2, 64, 2, copies, 2, rows_each))
    for m in range(copies):
        for k in range(2):
            out[m, 0, k, :, 0, m, k], out[m, 1, k, :, 0, m, k] = c, -s
            out[m, 0, k, :, 1, m, k], out[m, 1, k, :, 1, m, k] = s, c
    return out.reshape(copies * 256, 2 * copies * 2 * rows_each)


def cmul_const(a, ang):
    r, i = a
    n = round(ang / (math.pi / 16)) % 32
    if n == 0:
        return (r, i)
    if n == 8:
        return (-i, r)
    if n == 16:
        return (-r, -i)
    if n == 24:
        return (i, -r)
    h = math.sqrt(0.5)
    if n == 4:
        return ((r - i) * h, (r + i) * h)
    if n == 12:
        return ((r + i) * (-h), (r - i) * h)
    if n == 20:
        return ((i - r) * h, (r + i) * (-h))
    if n == 28:
        return ((r + i) * h, (i - r) * h)
    c, s = math.cos(n * math.pi / 16), math.sin(n * math.pi / 16)
    return (r * c - i * s, r * s + i * c)


def cadd(a, b):
    return (a[0] + b[0], a[1] + b[1])


def csub(a, b):
    return (a[0] - b[0], a[1] - b[1])


def fft_small(z, sign):
    n = len(z)
    if n == 1:
        return z
    if n == 2:
        return [cadd(z[0], z[1]), csub(z[0], z[1])]
    even, odd = fft_small(z[0::2], sign), fft_small(z[1::2], sign)
    out = [None] * n
    for k in range(n // 2):
        w = cmul_const(odd[k], sign * 2 * math.pi * k / n)
        out[k], out[k + n // 2] = cadd(even[k], w), csub(even[k], w)
    return out


def forward32(x):
    z = fft_small([(x[2 * m], x[2 * m + 1]) for m in range(16)], -1)
    ends = (z[0][0] + z[0][1], z[0][0] - z[0][1])
    rest = [None] * 16
    for k in range(1, 9):
        a, b = z[k], z[16 - k]
        even = (a[0] + b[0], a[1] - b[1])
        odd = (a[1] + b[1], b[0] - a[0])
        turned = cmul_const(odd, -2 * math.pi * k / 32)
        rest[k] = cadd(even, turned)
        if k < 8:
            other = csub(even, turned)
            rest[16 - k] = (other[0], -other[1])
    return ends, rest


def backward32(ends, rest):
    z = [None] * 16
    z[0] = (ends[0] + ends[1], ends[0] - ends[1])
    for k in range(1, 9):
        a, b = rest[k], rest[16 - k]
        even = (a[0] + b[0], a[1] - b[1])
        odd = cmul_const((a[0] - b[0], a[1] + b[1]), 2 * math.pi * k / 32)
        z[k] = (even[0] - odd[1], even[1] + odd[0])
        if k < 8:
            z[16 - k] = (even[0] + odd[1], odd[0] - even[1])
    z = fft_small(z, 1)
    out = []
    for m in range(16):
        out += [z[m][0], z[m][1]]
    return out


def split(x):
    high = x.astype(bf16)
    low = (x - high.astype(f32)).astype(bf16)
    return high, low


def mm(a, b, dims):
    return lax.dot_general(a, b, (dims, ((), ())), preferred_element_type=f32)


def dot_right(x, table, dims=((1,), (0,))):
    high, low = split(x)
    return mm(high, table[0], dims) + (mm(high, table[1], dims) + mm(low, table[0], dims))


def dot_left(table, x, dims=((1,), (0,))):
    high, low = split(x)
    return mm(table[0], high, dims) + (mm(table[0], low, dims) + mm(table[1], high, dims))


def pair(ref, *lead):
    return ref[(0,) + lead], ref[(1,) + lead]


def row_forward(x_ref, y_ref, tw_ref, fg_ref, fs_ref, put):
    def radix(step, _):
        rows = pl.ds(pl.multiple_of(step * 8, 8), 8)
        for h in range(2):
            lanes = pl.ds(128 * h, 128)
            x = [x_ref[rows, pl.ds(256 * q + 128 * h, 128)] for q in range(32)]
            ends, rest = forward32(x)
            y_ref[rows, pl.ds(128 * h, 128)] = ends[0]
            y_ref[rows, pl.ds(256 + 128 * h, 128)] = ends[1]
            for k in range(1, 16):
                c, s = tw_ref[0, k : k + 1, lanes], tw_ref[1, k : k + 1, lanes]
                r, i = rest[k]
                to = pl.ds(pl.multiple_of(k * 64 + step * 8, 8), 8)
                y_ref[to, pl.ds(128 * h, 128)] = r * c + i * s
                y_ref[to, pl.ds(256 + 128 * h, 128)] = i * c - r * s
        return 0

    lax.fori_loop(0, 8, radix, 0)

    def product(step, _):
        y = y_ref[pl.ds(pl.multiple_of(step * 256, 256), 256), :]
        out = dot_left(pair(fg_ref), y, ((1,), (1,)))
        put(2 * step, out[:, :128])
        put(2 * step + 1, out[:, 128:])
        return 0

    lax.fori_loop(0, 4, product, 0)
    return dot_left(pair(fs_ref), y_ref[:64, :], ((1,), (1,)))


def row_backward(get, u_ref, tw_ref, tables, special, rows_each, plen, finish):
    copies = 64 // rows_each

    def product(g, _):
        block = get(g)
        high, low = split(block)
        total = None
        hight, lowt = high.T, low.T
        for m in range(copies):
            part = slice(m * 2 * rows_each, (m + 1) * 2 * rows_each)
            th, tl = tables(m)
            one = mm(hight[part], th, ((1,), (0,))) + (mm(hight[part], tl, ((1,), (0,))) + mm(lowt[part], th, ((1,), (0,))))
            total = one if total is None else total + one
        u_ref[pl.ds(pl.multiple_of(g * 2 * rows_each, 2 * rows_each), 2 * rows_each), :] = total
        return 0

    lax.fori_loop(0, 8, product, 0)
    block = get(0)
    high, low = split(block)
    hight, lowt = high.T, low.T
    total = None
    for m in range(copies):
        part = slice(m * 2 * rows_each, (m + 1) * 2 * rows_each)
        th, tl = special(m)
        one = mm(hight[part], th, ((1,), (0,))) + (mm(hight[part], tl, ((1,), (0,))) + mm(lowt[part], th, ((1,), (0,))))
        total = one if total is None else total + one
    u_ref[:rows_each, :] = total[:rows_each]
    width = min(plen, 128)

    def radix(step, _):
        for h in range(plen // width):
            lanes = pl.ds(width * h, width)
            here = pl.ds(pl.multiple_of(step * 8, 8), 8)
            ends = (u_ref[here, lanes], u_ref[here, pl.ds(plen + width * h, width)])
            rest = [None] * 16
            for k in range(1, 16):
                c, s = tw_ref[0, k : k + 1, lanes], tw_ref[1, k : k + 1, lanes]
                at = pl.ds(pl.multiple_of(k * rows_each + step * 8, 8), 8)
                r, i = u_ref[at, lanes], u_ref[at, pl.ds(plen + width * h, width)]
                rest[k] = (r * c - i * s, r * s + i * c)
            finish(here, width * h, width, backward32(ends, rest))
        return 0

    lax.fori_loop(0, rows_each // 8, radix, 0)


def waves(me, i):
    g, e = me // 16, me % 16
    t = e + 16 * i
    lane = lax.broadcasted_iota(jnp.int32, (1, 128), 1)
    c = lane // 64
    k2 = 2 * g + c
    j2 = jnp.where(t % 2 == 1, -((t + 1) // 2), t // 2)
    kx = jnp.where(k2 == 0, 16 * t, k2 + 32 * j2)
    return kx


def wave_y():
    k = lax.broadcasted_iota(jnp.int32, (128, 128), 0)
    lane = lax.broadcasted_iota(jnp.int32, (128, 128), 1)
    j = lane % 64
    return k + 128 * jnp.where(j < 32, j, j - 64)


def column_forward(get, i, tc_ref, fo_ref, qf_ref):
    r = jnp.concatenate([get(i, 0), get(i, 1)], axis=0)
    out = dot_left(pair(fo_ref), r)
    r, im = out[:128], out[128:]
    c, s = tc_ref[0], tc_ref[1]
    turned = jnp.concatenate([r * c + im * s, im * c - r * s], axis=1)
    out = dot_right(turned, pair(qf_ref))
    return out[:, :128], out[:, 128:]


def column_backward(fields, tc_ref, bo_ref, qb_table):
    stacked = jnp.concatenate(fields, axis=0) if len(fields) > 1 else fields[0]
    u = dot_right(stacked, qb_table)
    c, s = tc_ref[0], tc_ref[1]
    cols = []
    for n in range(len(fields)):
        r, im = u[128 * n : 128 * n + 128, :128], u[128 * n : 128 * n + 128, 128:]
        cols.append(jnp.concatenate([r * c - im * s, r * s + im * c], axis=0))
    joined = jnp.concatenate(cols, axis=1) if len(cols) > 1 else cols[0]
    out = dot_left(pair(bo_ref), joined)
    return [out[:, 128 * n : 128 * n + 128] for n in range(len(fields))]


def spectral(me, i):
    kx = waves(me, i)
    ky = wave_y()
    kept = ((jnp.abs(kx) <= CUT) & (jnp.abs(ky) <= CUT)).astype(f32)
    factor = 2.0 * math.pi / N
    kappa_x, kappa_y = factor * kx.astype(f32), factor * ky.astype(f32)
    kappa_sq = kappa_x * kappa_x + kappa_y * kappa_y
    weight = jnp.where(kx == 0, 1.0, 2.0) / (float(N) * float(N))
    return kept, kappa_x, kappa_y, kappa_sq, weight, ky


def kernel_row_forward(x_ref, tw_ref, fg_ref, fs_ref, s_ref, y_ref):
    def put(g, value):
        s_ref[pl.ds(pl.multiple_of(g * 384, 384), 384), :] = value

    tail = row_forward(x_ref, y_ref, tw_ref, fg_ref, fs_ref, put)
    s_ref[:384, :64] = tail


def kernel_column_fields(r_ref, tc_ref, fo_ref, qf_ref, bo_ref, qb_ref, s_ref, vort_ref):
    me = lax.axis_index("band") * 4 + lax.axis_index("sub")

    def get(i, ri):
        return r_ref[pl.ds(ri * 12 + i, 128, stride=24), :]

    def slot(i, _):
        vr, vi = column_forward(get, i, tc_ref, fo_ref, qf_ref)
        kept, kappa_x, kappa_y, kappa_sq, weight, ky = spectral(me, i)
        vr, vi = vr * kept, vi * kept
        vort_ref[i, :, :128], vort_ref[i, :, 128:] = vr, vi
        positive = kappa_sq > 0
        inverse_sq = jnp.where(positive, 1.0 / jnp.where(positive, kappa_sq, 1.0), 0.0)
        sr, si = vr * inverse_sq, vi * inverse_sq
        kxw, kyw = kappa_x * weight, kappa_y * weight
        fields = [
            jnp.concatenate([-kyw * si, kyw * sr], axis=1),
            jnp.concatenate([kxw * si, -kxw * sr], axis=1),
            jnp.concatenate([-kxw * vi, kxw * vr], axis=1),
            jnp.concatenate([-kyw * vi, kyw * vr], axis=1),
        ]
        outs = column_backward(fields, tc_ref, bo_ref, pair(qb_ref))
        for f in range(4):
            for ri in range(2):
                s_ref[pl.ds(i * 8 + f * 2 + ri, 128, stride=88), :] = outs[f][128 * ri : 128 * ri + 128]
        return 0

    lax.fori_loop(0, 11, slot, 0)


def kernel_row_product(r_ref, tw_ref, gg_ref, gs_ref, fg_ref, fs_ref, s_ref, u_ref, a_ref, b_ref):
    me = lax.axis_index("band") * 4 + lax.axis_index("sub")

    def getter(f):
        def get(g):
            parts = [r_ref[pl.ds(g * 1408 + f * 2 + ri, 176, stride=8), :] for ri in range(2)]
            return jnp.concatenate(parts, axis=0)

        return get

    def keep(to):
        def finish(here, start, width, out):
            for q in range(32):
                to[here, pl.ds(256 * q + start, width)] = out[q]

        return finish

    def times(to):
        def finish(here, start, width, out):
            for q in range(32):
                at = pl.ds(256 * q + start, width)
                to[here, at] = to[here, at] * out[q]

        return finish

    def last(here, start, width, out):
        row = lax.broadcasted_iota(jnp.int32, (8, 128), 0) + (me * 64 + here.start)
        drive = forcing * jnp.sin((2.0 * math.pi * force_waves / N) * row.astype(f32))
        for q in range(32):
            at = pl.ds(256 * q + start, width)
            a_ref[here, at] = a_ref[here, at] + (b_ref[here, at] * out[q] - drive)

    tables, special = (lambda m: pair(gg_ref)), (lambda m: pair(gs_ref))
    for f, finish in ((0, keep(a_ref)), (2, times(a_ref)), (1, keep(b_ref)), (3, last)):
        row_backward(getter(f), u_ref, tw_ref, tables, special, 64, 256, finish)

    def put(g, value):
        s_ref[pl.ds(pl.multiple_of(g * 384, 384), 384), :] = value

    tail = row_forward(a_ref, u_ref, tw_ref, fg_ref, fs_ref, put)
    s_ref[:384, :64] = tail


def kernel_column_next(r_ref, vort_ref, tc_ref, tc1_ref, tc2_ref, fo_ref, qf_ref, bo_ref, qb_ref, q1_ref, q2_ref, s_ref, n_ref):
    me = lax.axis_index("band") * 4 + lax.axis_index("sub")

    def get(i, ri):
        return r_ref[pl.ds(ri * 12 + i, 128, stride=24), :]

    half_step = 0.5 * time_step

    def slot(i, _):
        ar, ai = column_forward(get, i, tc_ref, fo_ref, qf_ref)
        kept, kappa_x, kappa_y, kappa_sq, weight, ky = spectral(me, i)
        vr, vi = vort_ref[i, :, :128], vort_ref[i, :, 128:]
        ar, ai = ar * kept, ai * kept
        nr = (vr + half_step * (-ar - viscosity * kappa_sq * vr)) * weight
        ni = (vi + half_step * (-ai - viscosity * kappa_sq * vi)) * weight
        both = jnp.concatenate([nr, ni], axis=1)
        (out,) = column_backward([both], tc_ref, bo_ref, pair(qb_ref))
        for ri in range(2):
            s_ref[pl.ds(i + 11 * ri, 128, stride=32), :] = out[128 * ri : 128 * ri + 128]
        n_ref[i] = both
        return 0

    lax.fori_loop(0, 11, slot, 0)
    ky = wave_y()
    inside_one = jnp.concatenate([(jnp.abs(ky) < 2048).astype(f32)] * 2, axis=1)
    inside_two = jnp.concatenate([(jnp.abs(ky) < 1024).astype(f32)] * 2, axis=1)

    def first(m, _):
        block = jnp.concatenate([n_ref[2 * m] * inside_one, n_ref[2 * m + 1] * inside_one], axis=1)
        (out,) = column_backward([block], tc1_ref, bo_ref, pair(q1_ref))
        for ri in range(2):
            s_ref[pl.ds(22 + 2 * m + ri, 128, stride=32), :] = out[128 * ri : 128 * ri + 128]
        return 0

    lax.fori_loop(0, 4, first, 0)
    block = jnp.concatenate([n_ref[m] * inside_two for m in range(4)], axis=1)
    (out,) = column_backward([block], tc2_ref, bo_ref, pair(q2_ref))
    for ri in range(2):
        s_ref[pl.ds(30 + ri, 128, stride=32), :] = out[128 * ri : 128 * ri + 128]


def kernel_row_section(r_ref, tw_ref, g_ref, out_ref, u_ref):
    def get(g):
        return r_ref[pl.ds(pl.multiple_of(g * 512, 512), 512), :]

    def finish(here, start, width, out):
        for q in range(32):
            out_ref[here, pl.ds(256 * q + start, width)] = out[q]

    row_backward(get, u_ref, tw_ref, lambda m: pair(g_ref, 0), lambda m: pair(g_ref, 1), 64, 256, finish)


def kernel_row_coarse(r_ref, tw1_ref, tw2_ref, g1_ref, g2_ref, one_ref, two_ref, u1_ref, u2_ref):
    def get(g):
        return r_ref[pl.ds(pl.multiple_of(g * 512, 512), 512), :]

    def finish_one(here, start, width, out):
        for q in range(32):
            one_ref[here, pl.ds(128 * q + start, width)] = out[q]

    def finish_two(here, start, width, out):
        for q in range(16):
            two_ref[here, pl.ds(128 * q, 128)] = jnp.concatenate([out[2 * q], out[2 * q + 1]], axis=1)

    row_backward(get, u1_ref, tw1_ref, lambda m: pair(g1_ref, 0, m), lambda m: pair(g1_ref, 1, m), 32, 128, finish_one)
    row_backward(get, u2_ref, tw2_ref, lambda m: pair(g2_ref, 0, m), lambda m: pair(g2_ref, 1, m), 16, 64, finish_two)


def call(kernel, args, outs, scratch):
    vm = pl.BlockSpec(memory_space=pltpu.VMEM)
    shapes = [jax.ShapeDtypeStruct(s, f32) for s in outs]
    return pl.pallas_call(
        kernel,
        out_shape=shapes,
        in_specs=[vm] * len(args),
        out_specs=[vm] * len(outs),
        scratch_shapes=[pltpu.VMEM(s, f32) for s in scratch],
        compiler_params=pltpu.CompilerParams(vmem_limit_bytes=56 * 2**20),
    )(*args)


def exchange(x):
    rows = x.shape[0] // DEV
    out = lax.all_to_all(x.reshape(DEV, rows, 128), AXES, split_axis=0, concat_axis=0, tiled=True)
    return out.reshape(DEV * rows, 128)


def local(vorticity):
    fg, fs = forward_row_tables()
    gg, gs = backward_field_tables()
    g_full, g_one, g_two = backward_next_tables()
    tw, tw1, tw2 = row_twiddle(N), row_twiddle(N // 2), row_twiddle(N // 4)
    fo, bo = column_outer()
    tc, tc1, tc2 = column_twiddle(64, 2), column_twiddle(32, 4), column_twiddle(16, 8)
    inner = column_inner(64, 1, 1)
    qb, qf = halves(inner), halves(inner.T)
    q1, q2 = halves(column_inner(32, 2, 1)), halves(column_inner(16, 4, 1))

    (s1,) = call(kernel_row_forward, (vorticity, tw, fg, fs), [(3072, 128)], [(1024, 512)])
    r1 = exchange(s1)
    s2, vort = call(kernel_column_fields, (r1, tc, fo, qf, bo, qb), [(88 * 128, 128), (11, 128, 256)], [])
    r2 = exchange(s2)
    (s3,) = call(
        kernel_row_product,
        (r2, tw, gg, gs, fg, fs),
        [(3072, 128)],
        [(1024, 512), (64, N), (64, N)],
    )
    r3 = exchange(s3)
    (s4,) = call(
        kernel_column_next,
        (r3, vort, tc, tc1, tc2, fo, qf, bo, qb, q1, q2),
        [(32 * 128, 128)],
        [(11, 128, 256)],
    )
    r4 = exchange(s4)
    one, two = call(
        kernel_row_coarse, (r4, tw1, tw2, g_one, g_two), [(32, N // 2), (16, N // 4)], [(512, 256), (256, 128)]
    )
    coarse_one = lax.all_gather(one, "sub", axis=0, tiled=True)
    coarse_two = lax.all_gather(two, "sub", axis=0, tiled=True)
    (section,) = call(kernel_row_section, (r4, tw, g_full), [(64, N)], [(1024, 512)])
    return section, coarse_one, coarse_two


def solution(mesh):
    return jax.shard_map(
        local,
        mesh=mesh,
        in_specs=(P(AXES, None),),
        out_specs=(P(AXES, None), P("band", None), P("band", None)),
        check_vma=False,
    )
```

time: 817 us -> 311 us (0.38); the launches traced: 805 us -> 310 us
  local copies, waits for them, and re-layouts: 343 us -> 3.91 us
  matrix products: 219 us -> 0 us
  blocking collectives: 16.9 us -> 192 us
  Pallas kernels: 0 us -> 92.5 us
  starting transfers between devices: 88.7 us -> 0.04 us
  other arithmetic: 77.7 us -> 0 us
  waiting for transfers between devices: 44.1 us -> 6.85 us
    dot_general x58 -> x0, matrix products: 179 us -> none  [contract(): jnp.einsum(einsum_form, left_operand, right_operand, precision=lax.Precis...]
    all_to_all x0 -> x4, blocking collectives: none -> 177 us  [exchange(): lax.all_to_all(x.reshape(DEV, rows, 128), AXES, split_axis=0, concat_axis...]
    unnamed x146 -> x4, local copies, waits for them, and re-layouts: 134 us -> 3.91 us
    pallas_call x0 -> x6, Pallas kernels: none -> 92.5 us  [call(): pl.pallas_call(kernel, out_shape=shapes, in_specs=[vm] * len(args), out_s...]
    all_to_all x12 -> x0, starting transfers between devices: 88.7 us -> none  [the longest x2 15.5 us: local(): lax.all_to_all(entry_pair[1], ('band', 'sub'), split_axis=0, concat_axis=...]
    another operation x10 -> x0, local copies, waits for them, and re-layouts: 85.7 us -> none  [the longest x2 17.7 us: local(): grid_imag = grid_imag.reshape(length, 4, slab_width)]
    all_to_all x21 -> x0, local copies, waits for them, and re-layouts: 51 us -> none  [the longest x1 17.9 us: local(): lax.all_to_all(grid_imag, ('band', 'sub'), split_axis=0, concat_axis=2, t...]
    all_to_all x12 -> x0, waiting for transfers between devices: 44 us -> none  [the longest x2 12.3 us: local(): lax.all_to_all(entry_pair[1], ('band', 'sub'), split_axis=0, concat_axis=...]
  transfers between devices with their start and end apart: 13 -> 1, of which waited for: 8 -> 1; matrix products, arithmetic and copies ran while one was open for 32% -> 0% of each run, Pallas kernels for 0% -> 3%
where the time goes in v1:
time: 311 us; the launch traced here: 310 us
  blocking collectives  192 us (62%)
  Pallas kernels  92.5 us (30%)
  between operations  14 us (5%)
  waiting for transfers between devices  6.85 us (2%)
  local copies, waits for them, and re-layouts  3.91 us (1%)
    all_to_all x4, blocking collectives, exchange(): lax.all_to_all(x.reshape(DEV, rows, 128), AXES, split_axis=0, concat_axis...  177 us
    pallas_call x6, Pallas kernels, call(): pl.pallas_call(kernel, out_shape=shapes, in_specs=[vm] * len(args), out_s...  92.5 us
    all_gather x1, blocking collectives, local(): coarse_two = lax.all_gather(two, 'sub', axis=0, tiled=True)  15.6 us
    all_gather x1, waiting for transfers between devices, local(): coarse_one = lax.all_gather(one, 'sub', axis=0, tiled=True)  6.83 us
  transfers between devices with their start and end apart: 1, of which 1 were waited for; matrix products, arithmetic and copies ran while one was open for 0% of the time, Pallas kernels for 3%

profile of v1, /device:TPU:0, one launch (start us, length us, event | category | flops | bytes accessed | tf_op | source)
XLA Modules:
  0.0 309.8 jit_solution(12331667711467964044)
XLA Ops:
  7.2 0.0 all-gather.2.cloned.1.call-start
  7.2 6.5 %shard_map.211 = f32[3072,128]{1,0:T(8,128)} custom-call(f32[64,8192]{1,0:T(8,128)} %x_ref.1, f32[2,16,256]{2,1,0:T(8,128)} %constant.38.clone.tw_ref, bf16[2,384,512]{2,1,0:T(8,128)(2,1)} %constant.39.clone.fg_ref, bf16[2,384,512]{2,1,0:T(8,128)(2,1)} %constant.40.clone.fs_ref), custom_call_target="tpu_custom_call" | custom-call | tf_op jit(solution)/shard_map/pallas_call | solution.py:517
  13.7 35.8 %all_to_all.20 = f32[128,24,128]{2,1,0:T(8,128)} all-to-all(f32[128,24,128]{2,1,0:T(8,128)} %bitcast.14), channel_id=1, replica_groups=mesh['band'=32,'sub'=4] {'band','sub'}, dimensions={0} | all-to-all | bytes 3145728 | tf_op jit(solution)/shard_map/all_to_all | solution.py:529
  49.5 20.4 %shard_map.212 = (f32[11264,128]{1,0:T(8,128)}, f32[11,128,256]{2,1,0:T(8,128)}) custom-call(f32[3072,128]{1,0:T(8,128)} %bitcast.13, f32[2,128,128]{2,1,0:T(8,128)} %constant.41.clone.tc_ref, bf16[2,256,256]{2,1,0:T(8,128)(2,1)} %constant.42.clone.fo_ref, bf16[2,256,256]{2,1,0:T(8,128)(2,1)} %constant.43.clone.qf_ref, ...), custom_call_target="tpu_custom_call" | custom-call | tf_op jit(solution)/shard_map/pallas_call | solution.py:517
  70.0 75.2 %all_to_all.21 = f32[128,88,128]{2,1,0:T(8,128)} all-to-all(f32[128,88,128]{2,1,0:T(8,128)} %bitcast.16), channel_id=1, replica_groups=mesh['band'=32,'sub'=4] {'band','sub'}, dimensions={0} | all-to-all | bytes 11534336 | tf_op jit(solution)/shard_map/all_to_all | solution.py:529
  145.1 26.5 %shard_map.213 = f32[3072,128]{1,0:T(8,128)} custom-call(f32[11264,128]{1,0:T(8,128)} %bitcast.8, f32[2,16,256]{2,1,0:T(8,128)} %constant.38.clone.tw_ref, bf16[2,352,512]{2,1,0:T(8,128)(2,1)} %constant.46.clone.gg_ref, bf16[2,352,512]{2,1,0:T(8,128)(2,1)} %constant.47.clone.gs_ref, bf16[2,384,512]{2,1,0:T(8,128)(2,1)} %constant.39.clone.fg_ref, ...), custom_call_target="tpu_custom_call" | custom-call | tf_op jit(solution)/shard_map/pallas_call | solution.py:517
  171.7 30.1 %all_to_all.22 = f32[128,24,128]{2,1,0:T(8,128)} all-to-all(f32[128,24,128]{2,1,0:T(8,128)} %bitcast.12), channel_id=1, replica_groups=mesh['band'=32,'sub'=4] {'band','sub'}, dimensions={0} | all-to-all | bytes 3145728 | tf_op jit(solution)/shard_map/all_to_all | solution.py:529
  201.8 19.3 %shard_map.214 = f32[4096,128]{1,0:T(8,128)} custom-call(f32[3072,128]{1,0:T(8,128)} %bitcast.15, f32[11,128,256]{2,1,0:T(8,128)} %get-tuple-element.8.vort_ref, f32[2,128,128]{2,1,0:T(8,128)} %constant.41.clone.tc_ref, f32[2,128,128]{2,1,0:T(8,128)} %constant.48.clone.tc1_ref, f32[2,128,128]{2,1,0:T(8,128)} %constant.49.clone.tc2_ref, ...), custom_call_target="tpu_custom_call" | custom-call | tf_op jit(solution)/shard_map/pallas_call | solution.py:517
  221.1 35.7 %all_to_all.23 = f32[128,32,128]{2,1,0:T(8,128)} all-to-all(f32[128,32,128]{2,1,0:T(8,128)} %bitcast.11), channel_id=1, replica_groups=mesh['band'=32,'sub'=4] {'band','sub'}, dimensions={0} | all-to-all | bytes 4194304 | tf_op jit(solution)/shard_map/all_to_all | solution.py:529
  256.8 11.6 %shard_map.216 = (f32[32,4096]{1,0:T(8,128)}, f32[16,2048]{1,0:T(8,128)}) custom-call(f32[4096,128]{1,0:T(8,128)} %bitcast.9, f32[2,16,128]{2,1,0:T(8,128)} %constant.52.clone.tw1_ref, f32[2,16,64]{2,1,0:T(8,128)} %constant.53.clone.tw2_ref, bf16[2,2,2,512,256]{4,3,2,1,0:T(8,128)(2,1)} %constant.54.clone.g1_ref, ...), custom_call_target="tpu_custom_call" | custom-call | tf_op jit(solution)/shard_map/pallas_call | solution.py:517
  268.5 0.0 all-gather.2.cloned.1.call-update
  268.5 0.0 copy-start
  268.5 8.1 %shard_map.215 = f32[64,8192]{1,0:T(8,128)} custom-call(f32[4096,128]{1,0:T(8,128)} %bitcast.10, f32[2,16,256]{2,1,0:T(8,128)} %constant.38.clone.tw_ref, bf16[2,2,512,512]{3,2,1,0:T(8,128)(2,1)} %constant.56.clone.g_ref), custom_call_target="tpu_custom_call" | custom-call | tf_op jit(solution)/shard_map/pallas_call | solution.py:517
  276.6 0.0 copy-done
  276.6 15.6 %all_gather.7 = f32[64,2048]{1,0:T(8,128)S(1)} all-gather(f32[16,2048]{1,0:T(8,128)S(1)} %copy-done), channel_id=1, replica_groups=mesh['band'=32,'sub'=4] {'sub'}, dimensions={0}, use_global_device_ids=true | all-gather | bytes 655360 | tf_op jit(solution)/shard_map/all_gather | solution.py:566
  292.2 6.8 %all-gather.2.cloned.1.call-done = f32[128,4096]{1,0:T(8,128)} async-done(((f32[32,4096]{1,0:T(8,128)}), f32[128,4096]{1,0:T(8,128)}) %all-gather.2.cloned.1.call-update) | async-done | bytes 2097168 | tf_op jit(solution)/shard_map/all_gather | solution.py:565
  299.0 3.1 %copy.25 = f32[128,4096]{1,0:T(8,128)} copy(f32[128,4096]{1,0:T(8,128)} %all-gather.2.cloned.1.call-done) | data formatting | bytes 4194304
  302.2 0.8 copy.26
Async XLA Ops:
  7.2 291.9 %all-gather.2.cloned.1.call-start = ((), (), s32[]{:S(2)}) async-start(), calls=%async_computation.4 | async-start | bytes 2621440 | tf_op jit(solution)/shard_map/all_gather | solution.py:565
  268.5 8.1 %copy-start = (f32[16,2048]{1,0:T(8,128)S(1)}, f32[16,2048]{1,0:T(8,128)}, u32[]{:S(2)}) copy-start(f32[16,2048]{1,0:T(8,128)} %get-tuple-element.10) | copy-start | bytes 393220
Sparse Core Ops, SparseCore 0:
  268.6 30.4 all-gather.1

commit v2 on v1

v2 whole, which is shorter than its diff:
```python
import functools
import math

import jax
import jax.numpy as jnp
import ml_dtypes
import numpy as np
from jax import lax
from jax.experimental import pallas as pl
from jax.experimental.pallas import tpu as pltpu
from jax.sharding import PartitionSpec as P

time_step = 0.2
viscosity = 0.4
forcing = 1.0
force_waves = 4.0

N = 8192
CUT = N // 3
DEV = 128
AXES = ("band", "sub")
f32 = jnp.float32
bf16 = jnp.bfloat16


def halves(table):
    table = np.asarray(table, np.float64).astype(np.float32)
    high = table.astype(ml_dtypes.bfloat16)
    low = (table - high.astype(np.float32)).astype(ml_dtypes.bfloat16)
    return np.stack([high, low])


def wave_of(t):
    return np.where(t % 2 == 1, -(t + 1) // 2, t // 2)


def slot_index():
    e, i = np.meshgrid(np.arange(16), np.arange(11), indexing="ij")
    return e + 16 * i


def backward_row_values(t, length):
    plen = length // 32
    p = np.arange(plen)
    ang = 2 * np.pi * ((wave_of(t)[..., None] * p) % plen) / plen
    gen = np.zeros(t.shape + (2, 2, plen))
    gen[..., 0, 0, :], gen[..., 1, 0, :] = np.cos(ang), -np.sin(ang)
    gen[..., 0, 1, :], gen[..., 1, 1, :] = np.sin(ang), np.cos(ang)
    ang = 2 * np.pi * ((16 * t[..., None] * p) % length) / length
    odd = (t % 2 == 1)[..., None]
    spe = np.zeros(t.shape + (2, 2, plen))
    spe[..., 0, 0, :], spe[..., 1, 0, :] = np.where(odd, 0, np.cos(ang)), np.where(odd, 0, -np.sin(ang))
    spe[..., 0, 1, :], spe[..., 1, 1, :] = np.where(odd, np.cos(ang), 0), np.where(odd, -np.sin(ang), 0)
    return np.stack([gen, spe]).reshape((2,) + t.shape + (2, 2 * plen))


def forward_row_tables():
    t = slot_index()
    p = np.arange(256)
    out = np.zeros((2, 16, 2, 12, 2, 256))
    ang = 2 * np.pi * ((wave_of(t)[:, :, None] * p) % 256) / 256
    out[0, :, 0, :11, 0], out[0, :, 0, :11, 1] = np.cos(ang), np.sin(ang)
    out[0, :, 1, :11, 0], out[0, :, 1, :11, 1] = -np.sin(ang), np.cos(ang)
    ang = 2 * np.pi * ((16 * t[:, :, None] * p) % N) / N
    odd = (t % 2 == 1)[:, :, None]
    out[1, :, 0, :11, 0], out[1, :, 1, :11, 0] = np.where(odd, 0, np.cos(ang)), np.where(odd, 0, -np.sin(ang))
    out[1, :, 0, :11, 1], out[1, :, 1, :11, 1] = np.where(odd, np.cos(ang), 0), np.where(odd, -np.sin(ang), 0)
    out = out.reshape(2, 16, 2, 3, 4, 512).transpose(0, 3, 1, 2, 4, 5).reshape(2, 384, 512)
    return halves(out[0]), halves(out[1])


def backward_field_tables():
    v = backward_row_values(slot_index(), N).transpose(0, 3, 2, 1, 4)
    return halves(v[:, :, :8].reshape(2, 256, 512)), halves(v[:, :, 8:].reshape(2, 96, 512))


def backward_next_tables():
    t = slot_index()
    v = backward_row_values(t, N)
    full = np.zeros((2, 3, 16, 8, 512))
    for ri in range(2):
        for i in range(11):
            full[:, i // 4, :, ri * 4 + i % 4 if i < 8 else ri * 3 + i - 8] = v[:, :, i, ri]
    v1 = backward_row_values(t, N // 2)
    one = np.zeros((2, 2, 16, 8, 256))
    v2 = backward_row_values(t, N // 4)
    two = np.zeros((2, 4, 16, 8, 128))
    for ri in range(2):
        for i in range(8):
            one[:, i % 2, :, (i // 2) * 2 + ri] = v1[:, :, i, ri]
        for i in range(4):
            two[:, i, :, 6 + ri] = v2[:, :, i, ri]
    full = full.reshape(2, 384, 512)
    return (
        halves(full[:, :256]),
        halves(full[:, 256:]),
        halves(one.reshape(2, 2, 128, 256)),
        halves(two.reshape(2, 4, 128, 128)),
    )


def row_twiddle(length):
    plen = length // 32
    ang = 2 * np.pi * np.arange(16)[:, None] * np.arange(plen) / length
    return (0.5 * np.stack([np.cos(ang), np.sin(ang)])).astype(np.float32)


def column_outer():
    ang = 2 * np.pi * ((np.arange(128)[:, None] * np.arange(128)) % 128) / 128
    c, s = np.cos(ang), np.sin(ang)
    return halves(np.block([[c, s], [-s, c]])), halves(np.block([[c, -s], [s, c]]))


def column_twiddle(rows_each, copies):
    length = DEV * rows_each
    ang = 2 * np.pi * np.arange(128)[:, None] * np.arange(rows_each) / length
    return np.stack([np.tile(np.cos(ang), (1, copies)), np.tile(np.sin(ang), (1, copies))]).astype(np.float32)


def column_inner(rows_each, copies, sign):
    j = np.arange(64)
    signed = np.where(j < 32, j, j - 64)
    ang = 2 * np.pi * ((signed[:, None] * np.arange(rows_each)) % rows_each) / rows_each
    keep = ((signed >= -rows_each // 2) & (signed < rows_each // 2))[:, None]
    c, s = np.cos(ang) * keep, np.sin(ang) * keep
    out = np.zeros((copies, 2, 2, 64, 2, copies, 2, rows_each))
    for m in range(copies):
        for k in range(2):
            out[m, 0, k, :, 0, m, k], out[m, 1, k, :, 0, m, k] = c, -s
            out[m, 0, k, :, 1, m, k], out[m, 1, k, :, 1, m, k] = s, c
    return out.reshape(copies * 256, 2 * copies * 2 * rows_each)


def cmul_const(a, ang):
    r, i = a
    n = round(ang / (math.pi / 16)) % 32
    if n == 0:
        return (r, i)
    if n == 8:
        return (-i, r)
    if n == 16:
        return (-r, -i)
    if n == 24:
        return (i, -r)
    h = math.sqrt(0.5)
    if n == 4:
        return ((r - i) * h, (r + i) * h)
    if n == 12:
        return ((r + i) * (-h), (r - i) * h)
    if n == 20:
        return ((i - r) * h, (r + i) * (-h))
    if n == 28:
        return ((r + i) * h, (i - r) * h)
    c, s = math.cos(n * math.pi / 16), math.sin(n * math.pi / 16)
    return (r * c - i * s, r * s + i * c)


def cadd(a, b):
    return (a[0] + b[0], a[1] + b[1])


def csub(a, b):
    return (a[0] - b[0], a[1] - b[1])


def fft_small(z, sign):
    n = len(z)
    if n == 1:
        return z
    if n == 2:
        return [cadd(z[0], z[1]), csub(z[0], z[1])]
    even, odd = fft_small(z[0::2], sign), fft_small(z[1::2], sign)
    out = [None] * n
    for k in range(n // 2):
        w = cmul_const(odd[k], sign * 2 * math.pi * k / n)
        out[k], out[k + n // 2] = cadd(even[k], w), csub(even[k], w)
    return out


def forward32(x):
    z = fft_small([(x[2 * m], x[2 * m + 1]) for m in range(16)], -1)
    ends = (z[0][0] + z[0][1], z[0][0] - z[0][1])
    rest = [None] * 16
    for k in range(1, 9):
        a, b = z[k], z[16 - k]
        even = (a[0] + b[0], a[1] - b[1])
        odd = (a[1] + b[1], b[0] - a[0])
        turned = cmul_const(odd, -2 * math.pi * k / 32)
        rest[k] = cadd(even, turned)
        if k < 8:
            other = csub(even, turned)
            rest[16 - k] = (other[0], -other[1])
    return ends, rest


def backward32(ends, rest):
    z = [None] * 16
    z[0] = (ends[0] + ends[1], ends[0] - ends[1])
    for k in range(1, 9):
        a, b = rest[k], rest[16 - k]
        even = (a[0] + b[0], a[1] - b[1])
        odd = cmul_const((a[0] - b[0], a[1] + b[1]), 2 * math.pi * k / 32)
        z[k] = (even[0] - odd[1], even[1] + odd[0])
        if k < 8:
            z[16 - k] = (even[0] + odd[1], odd[0] - even[1])
    z = fft_small(z, 1)
    out = []
    for m in range(16):
        out += [z[m][0], z[m][1]]
    return out


def split(x):
    high = x.astype(bf16)
    low = (x - high.astype(f32)).astype(bf16)
    return high, low


def mm(a, b, dims):
    return lax.dot_general(a, b, (dims, ((), ())), preferred_element_type=f32)


def dot_right(x, table, dims=((1,), (0,))):
    high, low = split(x)
    return mm(high, table[0], dims) + (mm(high, table[1], dims) + mm(low, table[0], dims))


def dot_left(table, x, dims=((1,), (0,))):
    high, low = split(x)
    return mm(table[0], high, dims) + (mm(table[0], low, dims) + mm(table[1], high, dims))


def pair(ref, *lead):
    return ref[(0,) + lead], ref[(1,) + lead]


MESH = pl.DeviceIdType.MESH
half_step = 0.5 * time_step
NN = ((1,), (0,))


def rows8(n):
    return pl.ds(pl.multiple_of(n * 8, 8), 8)


def kernel(names, *refs):
    count = len(names)
    ins, rest = refs[: count + 1], refs[count + 1 :]
    x_hbm, table_hbm = ins[0], ins[1:]
    section_ref, one_ref, two_ref = rest[:3]
    (x_v, y_ref, s1, r1, s2, r2, u4, up, s3, r3, s4, r4, vort_ref, next_ref, one_v, two_v, u1, u2) = rest[3:21]
    tables = rest[21 : 21 + count]
    send_sem, recv_sem, own_sem, load_sem, gather_send, gather_recv, out_sem = rest[21 + count :]
    T = dict(zip(names, tables))

    band, sub = lax.axis_index("band"), lax.axis_index("sub")
    me = band * 4 + sub
    y, z, c = band // 8, (band // 2) % 4, band % 2

    def peer(off):
        x2 = (sub + off % 4) % 4
        c2 = (c + (off // 4) % 2) % 2
        z2 = (z + (off // 8) % 4) % 4
        y2 = (y + off // 32) % 4
        return (y2 * 4 + z2) * 2 + c2, x2

    def load(n):
        if n < 0:
            return pltpu.make_async_copy(x_hbm, x_v, load_sem.at[count])
        return pltpu.make_async_copy(table_hbm[n], tables[n], load_sem.at[n])

    load(-1).start()
    for n in range(count):
        load(n).start()

    barrier = pltpu.get_barrier_semaphore()

    def greet(n, _):
        pl.semaphore_signal(barrier, inc=1, device_id=peer(n), device_id_type=MESH)
        return 0

    lax.fori_loop(1, DEV, greet, 0)

    def send(src, dst, m, sem):
        pltpu.make_async_copy(src.at[m, rows8(me)], dst.at[m, rows8(me)], own_sem.at[sem]).start()

        def one(n, _):
            to = peer((n * 37) % DEV)
            pltpu.make_async_remote_copy(
                src_ref=src.at[m, rows8(to[0] * 4 + to[1])],
                dst_ref=dst.at[m, rows8(me)],
                send_sem=send_sem.at[sem],
                recv_sem=recv_sem.at[sem],
                device_id=to,
                device_id_type=MESH,
            ).start()
            return 0

        lax.fori_loop(1, DEV, one, 0)

    def whole(src, dst, m, sem):
        return pltpu.make_async_remote_copy(
            src_ref=src.at[m, pl.ds(0, 8 * (DEV - 1))],
            dst_ref=dst.at[m, pl.ds(0, 8 * (DEV - 1))],
            send_sem=send_sem.at[sem],
            recv_sem=recv_sem.at[sem],
            device_id=peer(1),
            device_id_type=MESH,
        )

    def arrive(src, dst, m, sem):
        pltpu.make_async_copy(src.at[m, rows8(me)], dst.at[m, rows8(me)], own_sem.at[sem]).wait()
        whole(src, dst, m, sem).wait_recv()

    def put_forward(step, x, lanes, h, rows):
        ends, rest = forward32(x)
        y_ref[rows, pl.ds(128 * h, 128)] = ends[0]
        y_ref[rows, pl.ds(256 + 128 * h, 128)] = ends[1]
        tw = T["tw"]
        for k in range(1, 16):
            cs, sn = tw[0, k : k + 1, lanes], tw[1, k : k + 1, lanes]
            r, i = rest[k]
            to = rows8(k * 8 + step)
            y_ref[to, pl.ds(128 * h, 128)] = r * cs + i * sn
            y_ref[to, pl.ds(256 + 128 * h, 128)] = i * cs - r * sn

    def row_products(s):
        def product(step, _):
            v = y_ref[pl.ds(pl.multiple_of(step * 256, 256), 256), :]
            out = dot_left(pair(T["fg"]), v, ((1,), (1,)))
            for g in range(2):
                to = pl.ds(pl.multiple_of((2 * step + g) * 128, 128), 128)
                for m in range(3):
                    s[m, to, :] = out[128 * m : 128 * m + 128, 128 * g : 128 * g + 128]
            return 0

        lax.fori_loop(0, 4, product, 0)
        tail = dot_left(pair(T["fs"]), y_ref[:64, :], ((1,), (1,)))
        for m in range(3):
            s[m, :128, :64] = tail[128 * m : 128 * m + 128]

    load(-1).wait()
    for n in range(3):
        load(n).wait()

    def radix_first(step, _):
        rows = rows8(step)
        for h in range(2):
            x = [x_v[rows, pl.ds(256 * q + 128 * h, 128)] for q in range(32)]
            put_forward(step, x, pl.ds(128 * h, 128), h, rows)
        return 0

    lax.fori_loop(0, 8, radix_first, 0)
    row_products(s1)
    pl.semaphore_wait(barrier, DEV - 1)
    for m in range(3):
        send(s1, r1, m, m)
    for n in range(3, count):
        load(n).wait()

    ky = wave_y()
    factor = 2.0 * math.pi / N
    kappa_y = factor * ky.astype(f32)
    kept_y = (jnp.abs(ky) <= CUT).astype(f32)

    def forward_four(r, m):
        blocks = []
        for ii in range(4):
            both = [r[m, pl.ds(ri * 4 + ii, 128, stride=8), :] for ri in range(2)]
            blocks.append(jnp.concatenate(both, axis=0))
        out = dot_left(pair(T["fo"]), jnp.concatenate(blocks, axis=1))
        cs, sn = T["tc"][0], T["tc"][1]
        turned = []
        for ii in range(4):
            re, im = out[:128, 128 * ii : 128 * ii + 128], out[128:, 128 * ii : 128 * ii + 128]
            turned.append(jnp.concatenate([re * cs + im * sn, im * cs - re * sn], axis=1))
        out = dot_right(jnp.concatenate(turned, axis=0), pair(T["qf"]))
        return [(out[128 * ii : 128 * ii + 128, :128], out[128 * ii : 128 * ii + 128, 128:]) for ii in range(4)]

    def x_part(i):
        g, e = me // 16, me % 16
        t = e + 16 * i
        lane = lax.broadcasted_iota(jnp.int32, (1, 128), 1)
        k2 = 2 * g + lane // 64
        j2 = jnp.where(t % 2 == 1, -((t + 1) // 2), t // 2)
        kx = jnp.where(k2 == 0, 16 * t, k2 + 32 * j2)
        kappa_x = factor * kx.astype(f32)
        weight = jnp.where(kx == 0, 1.0, 2.0) / (float(N) * float(N))
        return kappa_x, (jnp.abs(kx) <= CUT).astype(f32), weight

    for m in range(3):
        arrive(s1, r1, m, m)
        four = forward_four(r1, m)
        for ii in range(4):
            vort_ref[4 * m + ii, :, :128], vort_ref[4 * m + ii, :, 128:] = four[ii]

        def slot(i, _):
            kappa_x, kept_x, weight = x_part(i)
            kept = kept_y * kept_x
            kappa_sq = kappa_x * kappa_x + kappa_y * kappa_y
            vr, vi = vort_ref[i, :, :128] * kept, vort_ref[i, :, 128:] * kept
            vort_ref[i, :, :128], vort_ref[i, :, 128:] = vr, vi
            positive = kappa_sq > 0
            inverse_sq = jnp.where(positive, 1.0 / jnp.where(positive, kappa_sq, 1.0), 0.0)
            sr, si = vr * inverse_sq, vi * inverse_sq
            kxw, kyw = kappa_x * weight, kappa_y * weight
            fields = [
                jnp.concatenate([-kyw * si, kyw * sr], axis=1),
                jnp.concatenate([kxw * si, -kxw * sr], axis=1),
                jnp.concatenate([-kxw * vi, kxw * vr], axis=1),
                jnp.concatenate([-kyw * vi, kyw * vr], axis=1),
            ]
            outs = column_backward(fields, T["tc"], T["bo"], pair(T["qb"]))
            for f in range(4):
                for ri in range(2):
                    s2[i, pl.ds(f * 2 + ri, 128, stride=8), :] = outs[f][128 * ri : 128 * ri + 128]
            send(s2, r2, i, 3 + i)
            return 0

        lax.fori_loop(4 * m, min(4 * m + 4, 11), slot, 0)

    def gather_rows(f, g, slots):
        parts = []
        for ri in range(2):
            for i in slots:
                parts.append(r2[i, pl.ds(g * 128 + f * 2 + ri, 16, stride=8), :])
        high, low = split(jnp.concatenate(parts, axis=0))
        return high.T, low.T

    def three(a, th, tl):
        return mm(a[0], th, NN) + (mm(a[0], tl, NN) + mm(a[1], th, NN))

    for part, (slots, table) in enumerate(((range(8), "g8"), (range(8, 11), "g3"))):
        for i in slots:
            arrive(s2, r2, i, 3 + i)
        gt = T[table]

        def pairs(n, _):
            f, step = n // 4, n % 4
            a, b = gather_rows(f, 2 * step, slots), gather_rows(f, 2 * step + 1, slots)
            both = [jnp.concatenate([a[j], b[j]], axis=0) for j in range(2)]
            out = three(both, gt[0, 0], gt[1, 0])
            to = pl.ds(pl.multiple_of(step * 256, 256), 256)
            u4[f, to, :] = out if part == 0 else u4[f, to, :] + out
            return 0

        lax.fori_loop(0, 16, pairs, 0)

        def edge(f, _):
            a = gather_rows(f, 0, slots)
            out = three((a[0][:64], a[1][:64]), gt[0, 1], gt[1, 1])
            up[f] = out if part == 0 else up[f] + out
            return 0

        lax.fori_loop(0, 4, edge, 0)

    def grid_values(u, edge, tw, step, lanes, ims, stride):
        ends = (edge[rows8(step), lanes], edge[rows8(step), ims])
        rest = [None] * 16
        for k in range(1, 16):
            cs, sn = tw[0, k : k + 1, lanes], tw[1, k : k + 1, lanes]
            at = rows8(k * stride + step)
            r, i = u[at, lanes], u[at, ims]
            rest[k] = (r * cs - i * sn, r * sn + i * cs)
        return backward32(ends, rest)

    def radix_product(step, _):
        row = lax.broadcasted_iota(jnp.int32, (8, 128), 0) + (me * 64 + step * 8)
        drive = forcing * jnp.sin((2.0 * math.pi * force_waves / N) * row.astype(f32))
        for h in range(2):
            lanes, ims = pl.ds(128 * h, 128), pl.ds(256 + 128 * h, 128)
            vals = [None] * 4
            for f in (0, 2, 1, 3):
                vals[f] = grid_values(u4.at[f], up.at[f], T["tw"], step, lanes, ims, 8)
                if f == 2:
                    total = [vals[0][q] * vals[2][q] for q in range(32)]
            x = [total[q] + vals[1][q] * vals[3][q] - drive for q in range(32)]
            put_forward(step, x, lanes, h, rows8(step))
        return 0

    lax.fori_loop(0, 8, radix_product, 0)
    row_products(s3)
    for m in range(3):
        send(s3, r3, m, 14 + m)

    inside_one = jnp.concatenate([(jnp.abs(ky) < 2048).astype(f32)] * 2, axis=1)
    inside_two = jnp.concatenate([(jnp.abs(ky) < 1024).astype(f32)] * 2, axis=1)
    for m in range(3):
        arrive(s3, r3, m, 14 + m)
        four = forward_four(r3, m)
        blocks = []
        for ii in range(4):
            i = 4 * m + ii
            if i == 11:
                continue
            kappa_x, kept_x, weight = x_part(i)
            kept = kept_y * kept_x
            kappa_sq = kappa_x * kappa_x + kappa_y * kappa_y
            vr, vi = vort_ref[i, :, :128], vort_ref[i, :, 128:]
            ar, ai = four[ii][0] * kept, four[ii][1] * kept
            nr = (vr + half_step * (-ar - viscosity * kappa_sq * vr)) * weight
            ni = (vi + half_step * (-ai - viscosity * kappa_sq * vi)) * weight
            blocks.append(jnp.concatenate([nr, ni], axis=1))
            if i < 8:
                next_ref[i] = blocks[-1]
        outs = column_backward(blocks, T["tc"], T["bo"], pair(T["qb"]))
        for ii, out in enumerate(outs):
            for ri in range(2):
                to, r = (m, ri * 4 + ii) if m < 2 else (3, ri * 3 + ii)
                s4[to, pl.ds(r, 128, stride=8), :] = out[128 * ri : 128 * ri + 128]
        if m < 2:
            send(s4, r4, m, 17 + m)
        if m == 1:
            for n in range(4):
                block = jnp.concatenate([next_ref[2 * n] * inside_one, next_ref[2 * n + 1] * inside_one], axis=1)
                (out,) = column_backward([block], T["tc1"], T["bo"], pair(T["q1"]))
                for ri in range(2):
                    s4[2, pl.ds(2 * n + ri, 128, stride=8), :] = out[128 * ri : 128 * ri + 128]
            send(s4, r4, 2, 19)
        if m == 2:
            block = jnp.concatenate([next_ref[n] * inside_two for n in range(4)], axis=1)
            (out,) = column_backward([block], T["tc2"], T["bo"], pair(T["q2"]))
            for ri in range(2):
                s4[3, pl.ds(6 + ri, 128, stride=8), :] = out[128 * ri : 128 * ri + 128]
            send(s4, r4, 3, 20)

    def transposed(m, g):
        high, low = split(r4[m, pl.ds(pl.multiple_of(g * 128, 128), 128), :])
        return high.T, low.T

    def coarse(m, table, u, each):
        copies = 64 // each

        def value(g, kind):
            a = transposed(m, g)
            total = None
            for n in range(copies):
                part = slice(n * 2 * each, (n + 1) * 2 * each)
                out = three((a[0][part], a[1][part]), table[0, kind, n], table[1, kind, n])
                total = out if total is None else total + out
            return total

        def product(g, _):
            u[pl.ds(pl.multiple_of(g * 2 * each, 2 * each), 2 * each), :] = value(g, 0)
            return 0

        lax.fori_loop(0, 8, product, 0)
        u[:each, :] = value(0, 1)[:each]

    def spread(value, out, each, base):
        rows = pl.ds(pl.multiple_of(sub * each, each), each)
        pltpu.make_async_copy(value, out.at[rows], out_sem.at[base // 3]).start()
        for n in range(3):
            pltpu.make_async_remote_copy(
                src_ref=value,
                dst_ref=out.at[rows],
                send_sem=gather_send.at[base + n],
                recv_sem=gather_recv.at[base + n],
                device_id=(band, (sub + n + 1) % 4),
                device_id_type=MESH,
            ).start()

    def gathered(value, out, each, base):
        rows = pl.ds(pl.multiple_of(sub * each, each), each)
        pltpu.make_async_copy(value, out.at[rows], out_sem.at[base // 3]).wait()
        for n in range(3):
            copy = pltpu.make_async_remote_copy(
                src_ref=value,
                dst_ref=out.at[rows],
                send_sem=gather_send.at[base + n],
                recv_sem=gather_recv.at[base + n],
                device_id=(band, (sub + n + 1) % 4),
                device_id_type=MESH,
            )
            copy.wait_send()
            copy.wait_recv()

    arrive(s4, r4, 0, 17)
    arrive(s4, r4, 1, 18)
    u0, u0p = u4.at[0], up.at[0]

    def section_first(step, _):
        parts = [[transposed(m, 2 * step + g) for m in range(2)] for g in range(2)]
        both = [
            jnp.concatenate([jnp.concatenate([parts[g][0][j], parts[g][1][j]], axis=1) for g in range(2)], axis=0)
            for j in range(2)
        ]
        u0[pl.ds(pl.multiple_of(step * 256, 256), 256), :] = three(both, T["e8"][0, 0], T["e8"][1, 0])
        return 0

    lax.fori_loop(0, 4, section_first, 0)
    parts = [transposed(m, 0) for m in range(2)]
    both = [jnp.concatenate([parts[0][j][:64], parts[1][j][:64]], axis=1) for j in range(2)]
    u0p[...] = three(both, T["e8"][0, 1], T["e8"][1, 1])

    arrive(s4, r4, 2, 19)
    coarse(2, T["c1"], u1, 32)

    def radix_one(step, _):
        out = grid_values(u1, u1, T["tw1"], step, pl.ds(0, 128), pl.ds(128, 128), 4)
        for q in range(32):
            one_v[rows8(step), pl.ds(128 * q, 128)] = out[q]
        return 0

    lax.fori_loop(0, 4, radix_one, 0)
    spread(one_v, one_ref, 32, 0)

    arrive(s4, r4, 3, 20)
    coarse(3, T["c2"], u2, 16)

    def radix_two(step, _):
        out = grid_values(u2, u2, T["tw2"], step, pl.ds(0, 64), pl.ds(64, 64), 2)
        for q in range(16):
            two_v[rows8(step), pl.ds(128 * q, 128)] = jnp.concatenate([out[2 * q], out[2 * q + 1]], axis=1)
        return 0

    lax.fori_loop(0, 2, radix_two, 0)
    spread(two_v, two_ref, 16, 3)

    def section_last(step, _):
        a = [transposed(3, 2 * step + g) for g in range(2)]
        both = [jnp.concatenate([a[0][j], a[1][j]], axis=0) for j in range(2)]
        to = pl.ds(pl.multiple_of(step * 256, 256), 256)
        u0[to, :] = u0[to, :] + three(both, T["e3"][0, 0], T["e3"][1, 0])
        return 0

    lax.fori_loop(0, 4, section_last, 0)
    a = transposed(3, 0)
    u0p[...] = u0p[...] + three((a[0][:64], a[1][:64]), T["e3"][0, 1], T["e3"][1, 1])

    def radix_section(step, _):
        for h in range(2):
            lanes, ims = pl.ds(128 * h, 128), pl.ds(256 + 128 * h, 128)
            out = grid_values(u0, u0p, T["tw"], step, lanes, ims, 8)
            for q in range(32):
                x_v[rows8(step), pl.ds(256 * q + 128 * h, 128)] = out[q]
        return 0

    lax.fori_loop(0, 8, radix_section, 0)
    final = pltpu.make_async_copy(x_v, section_ref, out_sem.at[2])
    final.start()
    for m in range(3):
        whole(s1, r1, m, m).wait_send()
        whole(s3, r3, m, 14 + m).wait_send()
    for i in range(11):
        whole(s2, r2, i, 3 + i).wait_send()
    for m in range(4):
        whole(s4, r4, m, 17 + m).wait_send()
    gathered(one_v, one_ref, 32, 0)
    gathered(two_v, two_ref, 16, 3)
    final.wait()


def wave_y():
    k = lax.broadcasted_iota(jnp.int32, (128, 128), 0)
    lane = lax.broadcasted_iota(jnp.int32, (128, 128), 1)
    j = lane % 64
    return k + 128 * jnp.where(j < 32, j, j - 64)


def column_backward(fields, tc_ref, bo_ref, qb_table):
    stacked = jnp.concatenate(fields, axis=0) if len(fields) > 1 else fields[0]
    u = dot_right(stacked, qb_table)
    c, s = tc_ref[0], tc_ref[1]
    cols = []
    for n in range(len(fields)):
        r, im = u[128 * n : 128 * n + 128, :128], u[128 * n : 128 * n + 128, 128:]
        cols.append(jnp.concatenate([r * c - im * s, r * s + im * c], axis=0))
    joined = jnp.concatenate(cols, axis=1) if len(cols) > 1 else cols[0]
    out = dot_left(pair(bo_ref), joined)
    return [out[:, 128 * n : 128 * n + 128] for n in range(len(fields))]


def all_tables():
    fg, fs = forward_row_tables()
    g8, g3 = backward_field_tables()
    e8, e3, c1, c2 = backward_next_tables()
    fo, bo = column_outer()
    inner = column_inner(64, 1, 1)
    return {
        "tw": row_twiddle(N),
        "fg": fg,
        "fs": fs,
        "fo": fo,
        "tc": column_twiddle(64, 2),
        "qf": halves(inner.T),
        "bo": bo,
        "qb": halves(inner),
        "g8": g8,
        "g3": g3,
        "tc1": column_twiddle(32, 4),
        "tc2": column_twiddle(16, 8),
        "q1": halves(column_inner(32, 2, 1)),
        "q2": halves(column_inner(16, 4, 1)),
        "e8": e8,
        "e3": e3,
        "c1": c1,
        "c2": c2,
        "tw1": row_twiddle(N // 2),
        "tw2": row_twiddle(N // 4),
    }


def local(vorticity):
    tables = all_tables()
    names = tuple(tables)
    anywhere = pl.BlockSpec(memory_space=pl.ANY)
    shapes = [(64, N), (128, N // 2), (64, N // 4)]
    part = lambda n: (n, 8 * DEV, 128)
    scratch = [(64, N), (1024, 512), part(3), part(3), part(11), part(11), (4, 1024, 512), (4, 64, 512)]
    scratch += [part(3), part(3), part(4), part(4), (12, 128, 256), (8, 128, 256)]
    scratch += [(32, N // 2), (16, N // 4), (512, 256), (256, 128)]
    dma = pltpu.SemaphoreType.DMA
    section, one, two = pl.pallas_call(
        functools.partial(kernel, names),
        out_shape=[jax.ShapeDtypeStruct(s, f32) for s in shapes],
        in_specs=[anywhere] * (1 + len(names)),
        out_specs=[anywhere] * 3,
        scratch_shapes=[pltpu.VMEM(s, f32) for s in scratch]
        + [pltpu.VMEM(t.shape, t.dtype) for t in tables.values()]
        + [dma((21,)), dma((21,)), dma((21,)), dma((len(names) + 1,)), dma((6,)), dma((6,)), dma((3,))],
        compiler_params=pltpu.CompilerParams(
            collective_id=0, has_side_effects=True, vmem_limit_bytes=60 * 2**20
        ),
    )(vorticity, *[jnp.asarray(t) for t in tables.values()])
    return section, one, two


def solution(mesh):
    return jax.shard_map(
        local,
        mesh=mesh,
        in_specs=(P(AXES, None),),
        out_specs=(P(AXES, None), P("band", None), P("band", None)),
        check_vma=False,
    )
```

time: 311 us -> 216 us (0.69)
  blocking collectives: 192 us -> 0 us
  Pallas kernels: 92.5 us -> 209 us
  between operations: 14 us -> 0.65 us
  waiting for transfers between devices: 6.85 us -> 0 us
    all_to_all x4 -> x0, blocking collectives: 177 us -> none  [exchange(): lax.all_to_all(x.reshape(DEV, rows, 128), AXES, split_axis=0, concat_axis...]
    pallas_call x6 -> x1, Pallas kernels: 92.5 us -> 209 us  [local(): pl.pallas_call(functools.partial(kernel, names), out_shape=[jax.ShapeDtyp...]
    all_gather x1 -> x0, blocking collectives: 15.6 us -> none  [local(): coarse_two = lax.all_gather(two, 'sub', axis=0, tiled=True)]
    all_gather x1 -> x0, waiting for transfers between devices: 6.83 us -> none  [local(): coarse_one = lax.all_gather(one, 'sub', axis=0, tiled=True)]
  transfers between devices with their start and end apart: 1 -> 0, of which waited for: 1 -> 0; matrix products, arithmetic and copies ran while one was open for 0% -> 0% of each run, Pallas kernels for 3% -> 0%
where the time goes in v2:
time: 216 us; the launch traced here: 215 us
  Pallas kernels  209 us (97%)
  local copies, waits for them, and re-layouts  5.4 us (2%)
    pallas_call x1, Pallas kernels, local(): pl.pallas_call(functools.partial(kernel, names), out_shape=[jax.ShapeDtyp...  209 us
    unnamed x7, local copies, waits for them, and re-layouts  5.4 us

profile of v2, /device:TPU:0, one launch (start us, length us, event | category | flops | bytes accessed | tf_op | source)
XLA Modules:
  0.0 215.1 jit_solution(9087704123211171628)
XLA Ops:
  0.6 209.1 %shard_map.220 = (f32[64,8192]{1,0:T(8,128)}, f32[128,4096]{1,0:T(8,128)}, f32[64,2048]{1,0:T(8,128)}) custom-call(f32[64,8192]{1,0:T(8,128)} %refs_0_.1, f32[2,16,256]{2,1,0:T(8,128)} %constant.40.clone.refs_1_, bf16[2,384,512]{2,1,0:T(8,128)(2,1)} %constant.41.clone.refs_2_, bf16[2,384,512]{2,1,0:T(8,128)(2,1)} %constant.42.clone.refs_3_, ...), custom_call_target="tpu_custom_call" | custom-call | tf_op jit(solution)/shard_map/pallas_call | solution.py:714
  209.7 0.0 copy-start
  209.7 3.2 %copy.27 = f32[64,8192]{1,0:T(8,128)} copy(f32[64,8192]{1,0:T(8,128)} %get-tuple-element.6) | data formatting | bytes 4194304
  212.9 0.0 copy-done
  212.9 0.0 copy-start.1
  212.9 1.3 copy.28
  214.3 0.1 copy-done.1
  214.3 0.8 copy.29
Async XLA Ops:
  209.7 3.2 %copy-start = (f32[128,4096]{1,0:T(8,128)S(1)}, f32[128,4096]{1,0:T(8,128)}, u32[]{:S(2)}) copy-start(f32[128,4096]{1,0:T(8,128)} %get-tuple-element.7) | copy-start | bytes 6291460
  212.9 1.4 copy-start.1

commit v3 on v2

--- a/solution.py
+++ b/solution.py
@@ -54,6 +54,19 @@
     return np.stack([gen, spe]).reshape((2,) + t.shape + (2, 2 * plen))
 
 
+def thirds(table):
+    left = np.asarray(table, np.float64).astype(np.float32)
+    out = []
+    for _ in range(3):
+        out.append(left.astype(ml_dtypes.bfloat16))
+        left = left - out[-1].astype(np.float32)
+    return np.stack(out)
+
+
+def stack3(pair_of):
+    return np.concatenate([pair_of[0], pair_of[1], pair_of[0]], axis=1)
+
+
 def forward_row_tables():
     t = slot_index()
     p = np.arange(256)
@@ -65,13 +78,17 @@
     odd = (t % 2 == 1)[:, :, None]
     out[1, :, 0, :11, 0], out[1, :, 1, :11, 0] = np.where(odd, 0, np.cos(ang)), np.where(odd, 0, -np.sin(ang))
     out[1, :, 0, :11, 1], out[1, :, 1, :11, 1] = np.where(odd, np.cos(ang), 0), np.where(odd, -np.sin(ang), 0)
-    out = out.reshape(2, 16, 2, 3, 4, 512).transpose(0, 3, 1, 2, 4, 5).reshape(2, 384, 512)
-    return halves(out[0]), halves(out[1])
+    full = np.zeros((2, 3, 16, 8, 512))
+    for ri in range(2):
+        for i in range(11):
+            full[:, i // 4, :, ri * 4 + i % 4 if i < 8 else ri * 3 + i - 8] = out[:, :, ri, i].reshape(2, 16, 512)
+    full = np.moveaxis(thirds(full.reshape(2, 384, 512)), 0, 1).reshape(2, 1152, 512)
+    return full[0], full[1]
 
 
 def backward_field_tables():
     v = backward_row_values(slot_index(), N).transpose(0, 3, 2, 1, 4)
-    return halves(v[:, :, :8].reshape(2, 256, 512)), halves(v[:, :, 8:].reshape(2, 96, 512))
+    return halves(v[:, :, :8].reshape(2, 256, 512)), stack3(halves(v[:, :, 8:].reshape(2, 96, 512)))
 
 
 def backward_next_tables():
@@ -89,13 +106,13 @@
         for i in range(8):
             one[:, i % 2, :, (i // 2) * 2 + ri] = v1[:, :, i, ri]
         for i in range(4):
-            two[:, i, :, 6 + ri] = v2[:, :, i, ri]
+            two[:, i, :, ri] = v2[:, :, i, ri]
     full = full.reshape(2, 384, 512)
     return (
         halves(full[:, :256]),
         halves(full[:, 256:]),
-        halves(one.reshape(2, 2, 128, 256)),
-        halves(two.reshape(2, 4, 128, 128)),
+        halves(one.reshape(2, 256, 256)),
+        halves(two.reshape(2, 512, 128)),
     )
 
 
@@ -108,7 +125,7 @@
 def column_outer():
     ang = 2 * np.pi * ((np.arange(128)[:, None] * np.arange(128)) % 128) / 128
     c, s = np.cos(ang), np.sin(ang)
-    return halves(np.block([[c, s], [-s, c]])), halves(np.block([[c, -s], [s, c]]))
+    return np.block([[c, s], [-s, c]]), np.block([[c, -s], [s, c]])
 
 
 def column_twiddle(rows_each, copies):
@@ -257,12 +274,28 @@
     me = band * 4 + sub
     y, z, c = band // 8, (band // 2) % 4, band % 2
 
-    def peer(off):
-        x2 = (sub + off % 4) % 4
-        c2 = (c + (off // 4) % 2) % 2
-        z2 = (z + (off // 8) % 4) % 4
-        y2 = (y + off // 32) % 4
-        return (y2 * 4 + z2) * 2 + c2, x2
+    def wrap(v):
+        return jnp.where(v >= 4, v - 4, v)
+
+    xs, cs = [sub] + [wrap(sub + k) for k in range(1, 4)], [c, 1 - c]
+
+    def each_peer(act, first=0, last=16):
+        def group(dy, dz, skip):
+            for k in range(4):
+                base = (wrap(wrap(y + dy) + k) * 4 + wrap(wrap(z + dz) + k)) * 2
+                for d in range(2):
+                    if not (skip and k == 0 and d == 0):
+                        act(base + cs[d], xs[k])
+
+        if first == 0:
+            group(0, 0, True)
+
+        def body(w, _):
+            dy = w // 4
+            group(dy, w - 4 * dy, False)
+            return 0
+
+        lax.fori_loop(max(first, 1), last, body, 0)
 
     def load(n):
         if n < 0:
@@ -275,42 +308,44 @@
 
     barrier = pltpu.get_barrier_semaphore()
 
-    def greet(n, _):
-        pl.semaphore_signal(barrier, inc=1, device_id=peer(n), device_id_type=MESH)
-        return 0
-
-    lax.fori_loop(1, DEV, greet, 0)
-
-    def send(src, dst, m, sem):
-        pltpu.make_async_copy(src.at[m, rows8(me)], dst.at[m, rows8(me)], own_sem.at[sem]).start()
-
-        def one(n, _):
-            to = peer((n * 37) % DEV)
+    def greet(*to):
+        pl.semaphore_signal(barrier, inc=1, device_id=to, device_id_type=MESH)
+
+    each_peer(greet)
+
+    def rows_of(n, count):
+        return pl.ds(pl.multiple_of(n * 8, 8), count)
+
+    def send(src, dst, m, sem, each=8):
+        own = rows_of(me, each)
+        pltpu.make_async_copy(src.at[m, own], dst.at[m, own], own_sem.at[sem]).start()
+
+        def one(*to):
             pltpu.make_async_remote_copy(
-                src_ref=src.at[m, rows8(to[0] * 4 + to[1])],
-                dst_ref=dst.at[m, rows8(me)],
+                src_ref=src.at[m, rows_of(to[0] * 4 + to[1], each)],
+                dst_ref=dst.at[m, own],
                 send_sem=send_sem.at[sem],
                 recv_sem=recv_sem.at[sem],
                 device_id=to,
                 device_id_type=MESH,
             ).start()
-            return 0
-
-        lax.fori_loop(1, DEV, one, 0)
-
-    def whole(src, dst, m, sem):
+
+        each_peer(one)
+
+    def whole(src, dst, m, sem, each=8):
         return pltpu.make_async_remote_copy(
-            src_ref=src.at[m, pl.ds(0, 8 * (DEV - 1))],
-            dst_ref=dst.at[m, pl.ds(0, 8 * (DEV - 1))],
+            src_ref=src.at[m, pl.ds(0, each * (DEV - 1))],
+            dst_ref=dst.at[m, pl.ds(0, each * (DEV - 1))],
             send_sem=send_sem.at[sem],
             recv_sem=recv_sem.at[sem],
-            device_id=peer(1),
+            device_id=(band, xs[1]),
             device_id_type=MESH,
         )
 
-    def arrive(src, dst, m, sem):
-        pltpu.make_async_copy(src.at[m, rows8(me)], dst.at[m, rows8(me)], own_sem.at[sem]).wait()
-        whole(src, dst, m, sem).wait_recv()
+    def arrive(src, dst, m, sem, each=8):
+        own = rows_of(me, each)
+        pltpu.make_async_copy(src.at[m, own], dst.at[m, own], own_sem.at[sem]).wait()
+        whole(src, dst, m, sem, each).wait_recv()
 
     def put_forward(step, x, lanes, h, rows):
         ends, rest = forward32(x)
@@ -324,10 +359,18 @@
             y_ref[to, pl.ds(128 * h, 128)] = r * cs + i * sn
             y_ref[to, pl.ds(256 + 128 * h, 128)] = i * cs - r * sn
 
-    def row_products(s):
+    def row_products(s, r, base, pieces, ready):
+        def value(table, v):
+            total = None
+            for n, part in enumerate(split_n(v, pieces)):
+                out = mm(table[: 384 * (pieces - n)], part, ((1,), (1,)))
+                for k in range(pieces - n):
+                    one = out[384 * k : 384 * k + 384]
+                    total = one if total is None else total + one
+            return total
+
         def product(step, _):
-            v = y_ref[pl.ds(pl.multiple_of(step * 256, 256), 256), :]
-            out = dot_left(pair(T["fg"]), v, ((1,), (1,)))
+            out = value(T["fg"], y_ref[pl.ds(pl.multiple_of(step * 256, 256), 256), :])
             for g in range(2):
                 to = pl.ds(pl.multiple_of((2 * step + g) * 128, 128), 128)
                 for m in range(3):
@@ -335,9 +378,12 @@
             return 0
 
         lax.fori_loop(0, 4, product, 0)
-        tail = dot_left(pair(T["fs"]), y_ref[:64, :], ((1,), (1,)))
+        tail = value(T["fs"], y_ref[:64, :])
         for m in range(3):
             s[m, :128, :64] = tail[128 * m : 128 * m + 128]
+        ready()
+        for m in range(3):
+            send(s, r, m, base + m, 8 if m < 2 else 6)
 
     load(-1).wait()
     for n in range(3):
@@ -351,10 +397,7 @@
         return 0
 
     lax.fori_loop(0, 8, radix_first, 0)
-    row_products(s1)
-    pl.semaphore_wait(barrier, DEV - 1)
-    for m in range(3):
-        send(s1, r1, m, m)
+    row_products(s1, r1, 0, 3, lambda: pl.semaphore_wait(barrier, DEV - 1))
     for n in range(3, count):
         load(n).wait()
 
@@ -363,19 +406,21 @@
     kappa_y = factor * ky.astype(f32)
     kept_y = (jnp.abs(ky) <= CUT).astype(f32)
 
-    def forward_four(r, m):
-        blocks = []
-        for ii in range(4):
-            both = [r[m, pl.ds(ri * 4 + ii, 128, stride=8), :] for ri in range(2)]
+    def forward_four(r, m, pieces):
+        blocks, four = [], 4 if m < 2 else 3
+        for ii in range(four):
+            both = [r[m, pl.ds(ri * four + ii, 128, stride=8), :] for ri in range(2)]
             blocks.append(jnp.concatenate(both, axis=0))
-        out = dot_left(pair(T["fo"]), jnp.concatenate(blocks, axis=1))
+        parts = split_n(jnp.concatenate(blocks, axis=1), pieces)
+        out = sum(mm(T["fo"][k], parts[n], NN) for n in range(pieces) for k in range(pieces - n))
         cs, sn = T["tc"][0], T["tc"][1]
         turned = []
-        for ii in range(4):
+        for ii in range(four):
             re, im = out[:128, 128 * ii : 128 * ii + 128], out[128:, 128 * ii : 128 * ii + 128]
             turned.append(jnp.concatenate([re * cs + im * sn, im * cs - re * sn], axis=1))
-        out = dot_right(jnp.concatenate(turned, axis=0), pair(T["qf"]))
-        return [(out[128 * ii : 128 * ii + 128, :128], out[128 * ii : 128 * ii + 128, 128:]) for ii in range(4)]
+        parts = split_n(jnp.concatenate(turned, axis=0), pieces)
+        out = sum(mm(parts[n], T["qf"][k], NN) for n in range(pieces) for k in range(pieces - n))
+        return [(out[128 * ii : 128 * ii + 128, :128], out[128 * ii : 128 * ii + 128, 128:]) for ii in range(four)]
 
     def x_part(i):
         g, e = me // 16, me % 16
@@ -389,9 +434,9 @@
         return kappa_x, (jnp.abs(kx) <= CUT).astype(f32), weight
 
     for m in range(3):
-        arrive(s1, r1, m, m)
-        four = forward_four(r1, m)
-        for ii in range(4):
+        arrive(s1, r1, m, m, 8 if m < 2 else 6)
+        four = forward_four(r1, m, 3)
+        for ii in range(len(four)):
             vort_ref[4 * m + ii, :, :128], vort_ref[4 * m + ii, :, 128:] = four[ii]
 
         def slot(i, _):
@@ -424,8 +469,7 @@
         for ri in range(2):
             for i in slots:
                 parts.append(r2[i, pl.ds(g * 128 + f * 2 + ri, 16, stride=8), :])
-        high, low = split(jnp.concatenate(parts, axis=0))
-        return high.T, low.T
+        return split(jnp.concatenate(parts, axis=0))
 
     def three(a, th, tl):
         return mm(a[0], th, NN) + (mm(a[0], tl, NN) + mm(a[1], th, NN))
@@ -435,11 +479,17 @@
             arrive(s2, r2, i, 3 + i)
         gt = T[table]
 
+        def value(f, gs, kind, rows):
+            got = [gather_rows(f, g, slots) for g in gs]
+            if part == 0:
+                both = [jnp.concatenate([a[j].T[:rows] for a in got], axis=0) for j in range(2)]
+                return three(both, gt[0, kind], gt[1, kind])
+            both = [jnp.concatenate([a[0], a[0], a[1]], axis=0).T[:rows] for a in got]
+            return mm(jnp.concatenate(both, axis=0), gt[kind], NN)
+
         def pairs(n, _):
             f, step = n // 4, n % 4
-            a, b = gather_rows(f, 2 * step, slots), gather_rows(f, 2 * step + 1, slots)
-            both = [jnp.concatenate([a[j], b[j]], axis=0) for j in range(2)]
-            out = three(both, gt[0, 0], gt[1, 0])
+            out = value(f, (2 * step, 2 * step + 1), 0, 128)
             to = pl.ds(pl.multiple_of(step * 256, 256), 256)
             u4[f, to, :] = out if part == 0 else u4[f, to, :] + out
             return 0
@@ -447,8 +497,7 @@
         lax.fori_loop(0, 16, pairs, 0)
 
         def edge(f, _):
-            a = gather_rows(f, 0, slots)
-            out = three((a[0][:64], a[1][:64]), gt[0, 1], gt[1, 1])
+            out = value(f, (0,), 1, 64)
             up[f] = out if part == 0 else up[f] + out
             return 0
 
@@ -479,37 +528,36 @@
         return 0
 
     lax.fori_loop(0, 8, radix_product, 0)
-    row_products(s3)
-    for m in range(3):
-        send(s3, r3, m, 14 + m)
+    row_products(s3, r3, 14, 2, lambda: None)
 
     inside_one = jnp.concatenate([(jnp.abs(ky) < 2048).astype(f32)] * 2, axis=1)
     inside_two = jnp.concatenate([(jnp.abs(ky) < 1024).astype(f32)] * 2, axis=1)
+
+    def whole_blocks(m, blocks):
+        outs = column_backward(blocks, T["tc"], T["bo"], pair(T["qb"]))
+        for ii, out in enumerate(outs):
+            for ri in range(2):
+                to, r = (m, ri * 4 + ii) if m < 2 else (3, ri * 3 + ii)
+                s4[to, pl.ds(r, 128, stride=8), :] = out[128 * ri : 128 * ri + 128]
+
     for m in range(3):
-        arrive(s3, r3, m, 14 + m)
-        four = forward_four(r3, m)
+        arrive(s3, r3, m, 14 + m, 8 if m < 2 else 6)
         blocks = []
-        for ii in range(4):
+        for ii, (ar, ai) in enumerate(forward_four(r3, m, 2)):
             i = 4 * m + ii
-            if i == 11:
-                continue
             kappa_x, kept_x, weight = x_part(i)
             kept = kept_y * kept_x
             kappa_sq = kappa_x * kappa_x + kappa_y * kappa_y
             vr, vi = vort_ref[i, :, :128], vort_ref[i, :, 128:]
-            ar, ai = four[ii][0] * kept, four[ii][1] * kept
+            ar, ai = ar * kept, ai * kept
             nr = (vr + half_step * (-ar - viscosity * kappa_sq * vr)) * weight
             ni = (vi + half_step * (-ai - viscosity * kappa_sq * vi)) * weight
             blocks.append(jnp.concatenate([nr, ni], axis=1))
             if i < 8:
                 next_ref[i] = blocks[-1]
-        outs = column_backward(blocks, T["tc"], T["bo"], pair(T["qb"]))
-        for ii, out in enumerate(outs):
-            for ri in range(2):
-                to, r = (m, ri * 4 + ii) if m < 2 else (3, ri * 3 + ii)
-                s4[to, pl.ds(r, 128, stride=8), :] = out[128 * ri : 128 * ri + 128]
-        if m < 2:
-            send(s4, r4, m, 17 + m)
+        if m == 0:
+            whole_blocks(0, blocks)
+            send(s4, r4, 0, 17)
         if m == 1:
             for n in range(4):
                 block = jnp.concatenate([next_ref[2 * n] * inside_one, next_ref[2 * n + 1] * inside_one], axis=1)
@@ -517,63 +565,114 @@
                 for ri in range(2):
                     s4[2, pl.ds(2 * n + ri, 128, stride=8), :] = out[128 * ri : 128 * ri + 128]
             send(s4, r4, 2, 19)
-        if m == 2:
             block = jnp.concatenate([next_ref[n] * inside_two for n in range(4)], axis=1)
             (out,) = column_backward([block], T["tc2"], T["bo"], pair(T["q2"]))
             for ri in range(2):
-                s4[3, pl.ds(6 + ri, 128, stride=8), :] = out[128 * ri : 128 * ri + 128]
-            send(s4, r4, 3, 20)
-
-    def transposed(m, g):
-        high, low = split(r4[m, pl.ds(pl.multiple_of(g * 128, 128), 128), :])
+                s4[4, pl.ds(ri, 128, stride=8), :] = out[128 * ri : 128 * ri + 128]
+            send(s4, r4, 4, 21, 2)
+            whole_blocks(1, blocks)
+            send(s4, r4, 1, 18)
+        if m == 2:
+            whole_blocks(2, blocks)
+            send(s4, r4, 3, 20, 6)
+
+    def transposed(m, g, valid=8):
+        block = r4[m, pl.ds(pl.multiple_of(g * 128, 128), 128), :]
+        if valid < 8:
+            row = lax.broadcasted_iota(jnp.int32, (128, 128), 0) % 8
+            block = jnp.where(row < valid, block, 0.0)
+        high, low = split(block)
         return high.T, low.T
 
-    def coarse(m, table, u, each):
+    def coarse(m, table, u, each, valid):
         copies = 64 // each
 
-        def value(g, kind):
-            a = transposed(m, g)
-            total = None
-            for n in range(copies):
-                part = slice(n * 2 * each, (n + 1) * 2 * each)
-                out = three((a[0][part], a[1][part]), table[0, kind, n], table[1, kind, n])
-                total = out if total is None else total + out
-            return total
-
-        def product(g, _):
-            u[pl.ds(pl.multiple_of(g * 2 * each, 2 * each), 2 * each), :] = value(g, 0)
+        def value(gs, kind):
+            both = [[], []]
+            for g in gs:
+                a = transposed(m, g, valid)
+                for j in range(2):
+                    parts = [a[j][n * 2 * each : (n + 1) * 2 * each] for n in range(copies)]
+                    both[j].append(jnp.concatenate(parts, axis=1))
+            both = [jnp.concatenate(v, axis=0) for v in both]
+            return three(both, table[0, kind], table[1, kind])
+
+        def product(n, _):
+            out = value([4 * n + k for k in range(4)], 0)
+            u[pl.ds(pl.multiple_of(n * 8 * each, 8 * each), 8 * each), :] = out
             return 0
 
-        lax.fori_loop(0, 8, product, 0)
-        u[:each, :] = value(0, 1)[:each]
-
-    def spread(value, out, each, base):
-        rows = pl.ds(pl.multiple_of(sub * each, each), each)
-        pltpu.make_async_copy(value, out.at[rows], out_sem.at[base // 3]).start()
-        for n in range(3):
-            pltpu.make_async_remote_copy(
-                src_ref=value,
-                dst_ref=out.at[rows],
-                send_sem=gather_send.at[base + n],
-                recv_sem=gather_recv.at[base + n],
-                device_id=(band, (sub + n + 1) % 4),
-                device_id_type=MESH,
-            ).start()
-
-    def gathered(value, out, each, base):
-        rows = pl.ds(pl.multiple_of(sub * each, each), each)
-        pltpu.make_async_copy(value, out.at[rows], out_sem.at[base // 3]).wait()
-        for n in range(3):
-            copy = pltpu.make_async_remote_copy(
-                src_ref=value,
-                dst_ref=out.at[rows],
-                send_sem=gather_send.at[base + n],
-                recv_sem=gather_recv.at[base + n],
-                device_id=(band, (sub + n + 1) % 4),
+        lax.fori_loop(0, 2, product, 0)
+        u[:each, :] = value([0], 1)[:each]
+
+    right, left = (sub + 1) % 4, (sub + 3) % 4
+
+    def ring(value, out, each, base):
+        def rows(owner, start, size):
+            return out.at[pl.ds(pl.multiple_of(owner * each + start, 8), size)]
+
+        def remote(src, dst, to, sem):
+            return pltpu.make_async_remote_copy(
+                src_ref=src,
+                dst_ref=dst,
+                send_sem=gather_send.at[base + sem],
+                recv_sem=gather_recv.at[base + sem],
+                device_id=(band, to),
                 device_id_type=MESH,
             )
-            copy.wait_send()
-            copy.wait_recv()
+
+        mine = rows(sub, 0, each)
+        own = pltpu.make_async_copy(value, mine, out_sem.at[base // 4])
+        first = [remote(value, mine, right, 0), remote(value, mine, left, 1)]
+        half = each // 2
+        a, b = rows(left, 0, half), rows(right, half, half)
+        second = [remote(a, a, right, 2), remote(b, b, left, 3)]
+
+        def start():
+            own.start()
+            for copy in first:
+                copy.start()
+
+        def forward():
+            for n in range(2):
+                first[n].wait_recv()
+                second[n].start()
+
+        def finish():
+            own.wait()
+            for copy in first:
+                copy.wait_send()
+            for copy in second:
+                copy.wait_send()
+                copy.wait_recv()
+
+        return start, forward, finish
+
+    ring_one, ring_two = ring(one_v, one_ref, 32, 0), ring(two_v, two_ref, 16, 4)
+
+    arrive(s4, r4, 2, 19)
+    coarse(2, T["c1"], u1, 32, 8)
+
+    def radix_one(step, _):
+        out = grid_values(u1, u1, T["tw1"], step, pl.ds(0, 128), pl.ds(128, 128), 4)
+        for q in range(32):
+            one_v[rows8(step), pl.ds(128 * q, 128)] = out[q]
+        return 0
+
+    lax.fori_loop(0, 4, radix_one, 0)
+    ring_one[0]()
+
+    arrive(s4, r4, 4, 21, 2)
+    coarse(4, T["c2"], u2, 16, 2)
+
+    def radix_two(step, _):
+        out = grid_values(u2, u2, T["tw2"], step, pl.ds(0, 64), pl.ds(64, 64), 2)
+        for q in range(16):
+            two_v[rows8(step), pl.ds(128 * q, 128)] = jnp.concatenate([out[2 * q], out[2 * q + 1]], axis=1)
+        return 0
+
+    lax.fori_loop(0, 2, radix_two, 0)
+    ring_two[0]()
 
     arrive(s4, r4, 0, 17)
     arrive(s4, r4, 1, 18)
@@ -592,40 +691,20 @@
     parts = [transposed(m, 0) for m in range(2)]
     both = [jnp.concatenate([parts[0][j][:64], parts[1][j][:64]], axis=1) for j in range(2)]
     u0p[...] = three(both, T["e8"][0, 1], T["e8"][1, 1])
-
-    arrive(s4, r4, 2, 19)
-    coarse(2, T["c1"], u1, 32)
-
-    def radix_one(step, _):
-        out = grid_values(u1, u1, T["tw1"], step, pl.ds(0, 128), pl.ds(128, 128), 4)
-        for q in range(32):
-            one_v[rows8(step), pl.ds(128 * q, 128)] = out[q]
-        return 0
-
-    lax.fori_loop(0, 4, radix_one, 0)
-    spread(one_v, one_ref, 32, 0)
-
-    arrive(s4, r4, 3, 20)
-    coarse(3, T["c2"], u2, 16)
-
-    def radix_two(step, _):
-        out = grid_values(u2, u2, T["tw2"], step, pl.ds(0, 64), pl.ds(64, 64), 2)
-        for q in range(16):
-            two_v[rows8(step), pl.ds(128 * q, 128)] = jnp.concatenate([out[2 * q], out[2 * q + 1]], axis=1)
-        return 0
-
-    lax.fori_loop(0, 2, radix_two, 0)
-    spread(two_v, two_ref, 16, 3)
+    ring_one[1]()
+    ring_two[1]()
+
+    arrive(s4, r4, 3, 20, 6)
 
     def section_last(step, _):
-        a = [transposed(3, 2 * step + g) for g in range(2)]
+        a = [transposed(3, 2 * step + g, 6) for g in range(2)]
         both = [jnp.concatenate([a[0][j], a[1][j]], axis=0) for j in range(2)]
         to = pl.ds(pl.multiple_of(step * 256, 256), 256)
         u0[to, :] = u0[to, :] + three(both, T["e3"][0, 0], T["e3"][1, 0])
         return 0
 
     lax.fori_loop(0, 4, section_last, 0)
-    a = transposed(3, 0)
+    a = transposed(3, 0, 6)
     u0p[...] = u0p[...] + three((a[0][:64], a[1][:64]), T["e3"][0, 1], T["e3"][1, 1])
 
     def radix_section(step, _):
@@ -640,15 +719,23 @@
     final = pltpu.make_async_copy(x_v, section_ref, out_sem.at[2])
     final.start()
     for m in range(3):
-        whole(s1, r1, m, m).wait_send()
-        whole(s3, r3, m, 14 + m).wait_send()
+        whole(s1, r1, m, m, 8 if m < 2 else 6).wait_send()
+        whole(s3, r3, m, 14 + m, 8 if m < 2 else 6).wait_send()
     for i in range(11):
         whole(s2, r2, i, 3 + i).wait_send()
-    for m in range(4):
-        whole(s4, r4, m, 17 + m).wait_send()
-    gathered(one_v, one_ref, 32, 0)
-    gathered(two_v, two_ref, 16, 3)
+    for m, each in enumerate((8, 8, 8, 6, 2)):
+        whole(s4, r4, m, 17 + m, each).wait_send()
+    ring_one[2]()
+    ring_two[2]()
     final.wait()
+
+
+def split_n(x, pieces):
+    out = []
+    for _ in range(pieces):
+        out.append(x.astype(bf16))
+        x = x - out[-1].astype(f32)
+    return out
 
 
 def wave_y():
@@ -675,16 +762,16 @@
     fg, fs = forward_row_tables()
     g8, g3 = backward_field_tables()
     e8, e3, c1, c2 = backward_next_tables()
-    fo, bo = column_outer()
+    outer = column_outer()
     inner = column_inner(64, 1, 1)
     return {
         "tw": row_twiddle(N),
         "fg": fg,
         "fs": fs,
-        "fo": fo,
+        "fo": thirds(outer[0]),
         "tc": column_twiddle(64, 2),
-        "qf": halves(inner.T),
-        "bo": bo,
+        "qf": thirds(inner.T),
+        "bo": halves(outer[1]),
         "qb": halves(inner),
         "g8": g8,
         "g3": g3,
@@ -708,7 +795,7 @@
     shapes = [(64, N), (128, N // 2), (64, N // 4)]
     part = lambda n: (n, 8 * DEV, 128)
     scratch = [(64, N), (1024, 512), part(3), part(3), part(11), part(11), (4, 1024, 512), (4, 64, 512)]
-    scratch += [part(3), part(3), part(4), part(4), (12, 128, 256), (8, 128, 256)]
+    scratch += [part(3), part(3), part(5), part(5), (12, 128, 256), (8, 128, 256)]
     scratch += [(32, N // 2), (16, N // 4), (512, 256), (256, 128)]
     dma = pltpu.SemaphoreType.DMA
     section, one, two = pl.pallas_call(
@@ -718,7 +805,7 @@
         out_specs=[anywhere] * 3,
         scratch_shapes=[pltpu.VMEM(s, f32) for s in scratch]
         + [pltpu.VMEM(t.shape, t.dtype) for t in tables.values()]
-        + [dma((21,)), dma((21,)), dma((21,)), dma((len(names) + 1,)), dma((6,)), dma((6,)), dma((3,))],
+        + [dma((22,)), dma((22,)), dma((22,)), dma((len(names) + 1,)), dma((8,)), dma((8,)), dma((3,))],
         compiler_params=pltpu.CompilerParams(
             collective_id=0, has_side_effects=True, vmem_limit_bytes=60 * 2**20
         ),

time: 216 us -> 177 us (0.82)
  Pallas kernels: 209 us -> 171 us
    pallas_call x1, Pallas kernels: 209 us -> 171 us  [local(): pl.pallas_call(functools.partial(kernel, names), out_shape=[jax.ShapeDtyp...]
where the time goes in v3:
time: 177 us
  Pallas kernels  171 us (97%)
  local copies, waits for them, and re-layouts  5.4 us (3%)
    pallas_call x1, Pallas kernels, local(): pl.pallas_call(functools.partial(kernel, names), out_shape=[jax.ShapeDtyp...  171 us
    unnamed x7, local copies, waits for them, and re-layouts  5.4 us

profile of v3, /device:TPU:0, one launch (start us, length us, event | category | flops | bytes accessed | tf_op | source)
XLA Modules:
  0.0 176.7 jit_solution(13459842984576524961)
XLA Ops:
  0.6 170.6 %shard_map.220 = (f32[64,8192]{1,0:T(8,128)}, f32[128,4096]{1,0:T(8,128)}, f32[64,2048]{1,0:T(8,128)}) custom-call(f32[64,8192]{1,0:T(8,128)} %refs_0_.1, f32[2,16,256]{2,1,0:T(8,128)} %constant.40.clone.refs_1_, bf16[1152,512]{1,0:T(8,128)(2,1)} %constant.41.clone.refs_2_, bf16[1152,512]{1,0:T(8,128)(2,1)} %constant.42.clone.refs_3_, ...), custom_call_target="tpu_custom_call" | custom-call | tf_op jit(solution)/shard_map/pallas_call | solution.py:801
  171.3 0.0 copy-start
  171.3 3.2 %copy.27 = f32[64,8192]{1,0:T(8,128)} copy(f32[64,8192]{1,0:T(8,128)} %get-tuple-element.6) | data formatting | bytes 4194304
  174.5 0.0 copy-done
  174.5 0.0 copy-start.1
  174.5 1.3 copy.28
  175.8 0.1 copy-done.1
  175.9 0.8 copy.29
Async XLA Ops:
  171.3 3.2 %copy-start = (f32[128,4096]{1,0:T(8,128)S(1)}, f32[128,4096]{1,0:T(8,128)}, u32[]{:S(2)}) copy-start(f32[128,4096]{1,0:T(8,128)} %get-tuple-element.7) | copy-start | bytes 6291460
  174.5 1.4 copy-start.1

commit v4 on v3

--- a/solution.py
+++ b/solution.py
@@ -386,8 +386,7 @@
             send(s, r, m, base + m, 8 if m < 2 else 6)
 
     load(-1).wait()
-    for n in range(3):
-        load(n).wait()
+    load(0).wait()
 
     def radix_first(step, _):
         rows = rows8(step)
@@ -397,6 +396,8 @@
         return 0
 
     lax.fori_loop(0, 8, radix_first, 0)
+    load(1).wait()
+    load(2).wait()
     row_products(s1, r1, 0, 3, lambda: pl.semaphore_wait(barrier, DEV - 1))
     for n in range(3, count):
         load(n).wait()
@@ -479,8 +480,8 @@
             arrive(s2, r2, i, 3 + i)
         gt = T[table]
 
-        def value(f, gs, kind, rows):
-            got = [gather_rows(f, g, slots) for g in gs]
+        def value(fgs, kind, rows):
+            got = [gather_rows(f, g, slots) for f, g in fgs]
             if part == 0:
                 both = [jnp.concatenate([a[j].T[:rows] for a in got], axis=0) for j in range(2)]
                 return three(both, gt[0, kind], gt[1, kind])
@@ -488,20 +489,18 @@
             return mm(jnp.concatenate(both, axis=0), gt[kind], NN)
 
         def pairs(n, _):
-            f, step = n // 4, n % 4
-            out = value(f, (2 * step, 2 * step + 1), 0, 128)
-            to = pl.ds(pl.multiple_of(step * 256, 256), 256)
+            f, step = n // 2, n % 2
+            out = value([(f, 4 * step + k) for k in range(4)], 0, 128)
+            to = pl.ds(pl.multiple_of(step * 512, 512), 512)
             u4[f, to, :] = out if part == 0 else u4[f, to, :] + out
             return 0
 
-        lax.fori_loop(0, 16, pairs, 0)
-
-        def edge(f, _):
-            out = value(f, (0,), 1, 64)
+        lax.fori_loop(0, 8, pairs, 0)
+
+        edge = value([(f, 0) for f in range(4)], 1, 64)
+        for f in range(4):
+            out = edge[64 * f : 64 * f + 64]
             up[f] = out if part == 0 else up[f] + out
-            return 0
-
-        lax.fori_loop(0, 4, edge, 0)
 
     def grid_values(u, edge, tw, step, lanes, ims, stride):
         ends = (edge[rows8(step), lanes], edge[rows8(step), ims])
@@ -559,9 +558,11 @@
             whole_blocks(0, blocks)
             send(s4, r4, 0, 17)
         if m == 1:
-            for n in range(4):
-                block = jnp.concatenate([next_ref[2 * n] * inside_one, next_ref[2 * n + 1] * inside_one], axis=1)
-                (out,) = column_backward([block], T["tc1"], T["bo"], pair(T["q1"]))
+            pairs_of = [
+                jnp.concatenate([next_ref[2 * n] * inside_one, next_ref[2 * n + 1] * inside_one], axis=1)
+                for n in range(4)
+            ]
+            for n, out in enumerate(column_backward(pairs_of, T["tc1"], T["bo"], pair(T["q1"]))):
                 for ri in range(2):
                     s4[2, pl.ds(2 * n + ri, 128, stride=8), :] = out[128 * ri : 128 * ri + 128]
             send(s4, r4, 2, 19)
@@ -679,15 +680,15 @@
     u0, u0p = u4.at[0], up.at[0]
 
     def section_first(step, _):
-        parts = [[transposed(m, 2 * step + g) for m in range(2)] for g in range(2)]
+        parts = [[transposed(m, 4 * step + g) for m in range(2)] for g in range(4)]
         both = [
-            jnp.concatenate([jnp.concatenate([parts[g][0][j], parts[g][1][j]], axis=1) for g in range(2)], axis=0)
+            jnp.concatenate([jnp.concatenate([parts[g][0][j], parts[g][1][j]], axis=1) for g in range(4)], axis=0)
             for j in range(2)
         ]
-        u0[pl.ds(pl.multiple_of(step * 256, 256), 256), :] = three(both, T["e8"][0, 0], T["e8"][1, 0])
+        u0[pl.ds(pl.multiple_of(step * 512, 512), 512), :] = three(both, T["e8"][0, 0], T["e8"][1, 0])
         return 0
 
-    lax.fori_loop(0, 4, section_first, 0)
+    lax.fori_loop(0, 2, section_first, 0)
     parts = [transposed(m, 0) for m in range(2)]
     both = [jnp.concatenate([parts[0][j][:64], parts[1][j][:64]], axis=1) for j in range(2)]
     u0p[...] = three(both, T["e8"][0, 1], T["e8"][1, 1])
@@ -697,13 +698,13 @@
     arrive(s4, r4, 3, 20, 6)
 
     def section_last(step, _):
-        a = [transposed(3, 2 * step + g, 6) for g in range(2)]
-        both = [jnp.concatenate([a[0][j], a[1][j]], axis=0) for j in range(2)]
-        to = pl.ds(pl.multiple_of(step * 256, 256), 256)
+        a = [transposed(3, 4 * step + g, 6) for g in range(4)]
+        both = [jnp.concatenate([v[j] for v in a], axis=0) for j in range(2)]
+        to = pl.ds(pl.multiple_of(step * 512, 512), 512)
         u0[to, :] = u0[to, :] + three(both, T["e3"][0, 0], T["e3"][1, 0])
         return 0
 
-    lax.fori_loop(0, 4, section_last, 0)
+    lax.fori_loop(0, 2, section_last, 0)
     a = transposed(3, 0, 6)
     u0p[...] = u0p[...] + three((a[0][:64], a[1][:64]), T["e3"][0, 1], T["e3"][1, 1])
 

time: 177 us -> 174 us (0.983)
  Pallas kernels: 171 us -> 168 us
    pallas_call x1, Pallas kernels: 171 us -> 168 us  [local(): pl.pallas_call(functools.partial(kernel, names), out_shape=[jax.ShapeDtyp...]
where the time goes in v4:
time: 174 us
  Pallas kernels  168 us (97%)
  local copies, waits for them, and re-layouts  5.4 us (3%)
    pallas_call x1, Pallas kernels, local(): pl.pallas_call(functools.partial(kernel, names), out_shape=[jax.ShapeDtyp...  168 us
    unnamed x7, local copies, waits for them, and re-layouts  5.4 us

profile of v4, /device:TPU:0, one launch (start us, length us, event | category | flops | bytes accessed | tf_op | source)
XLA Modules:
  0.0 173.9 jit_solution(278321559290130303)
XLA Ops:
  0.6 167.9 %shard_map.220 = (f32[64,8192]{1,0:T(8,128)}, f32[128,4096]{1,0:T(8,128)}, f32[64,2048]{1,0:T(8,128)}) custom-call(f32[64,8192]{1,0:T(8,128)} %refs_0_.1, f32[2,16,256]{2,1,0:T(8,128)} %constant.40.clone.refs_1_, bf16[1152,512]{1,0:T(8,128)(2,1)} %constant.41.clone.refs_2_, bf16[1152,512]{1,0:T(8,128)(2,1)} %constant.42.clone.refs_3_, ...), custom_call_target="tpu_custom_call" | custom-call | tf_op jit(solution)/shard_map/pallas_call | solution.py:802
  168.5 0.0 copy-start
  168.5 3.2 %copy.27 = f32[64,8192]{1,0:T(8,128)} copy(f32[64,8192]{1,0:T(8,128)} %get-tuple-element.6) | data formatting | bytes 4194304
  171.7 0.0 copy-done
  171.7 0.0 copy-start.1
  171.7 1.3 copy.28
  173.1 0.1 copy-done.1
  173.1 0.8 copy.29
Async XLA Ops:
  168.5 3.2 %copy-start = (f32[128,4096]{1,0:T(8,128)S(1)}, f32[128,4096]{1,0:T(8,128)}, u32[]{:S(2)}) copy-start(f32[128,4096]{1,0:T(8,128)} %get-tuple-element.7) | copy-start | bytes 6291460
  171.7 1.4 copy-start.1

commit v5 on v4

--- a/solution.py
+++ b/solution.py
@@ -82,7 +82,9 @@
     for ri in range(2):
         for i in range(11):
             full[:, i // 4, :, ri * 4 + i % 4 if i < 8 else ri * 3 + i - 8] = out[:, :, ri, i].reshape(2, 16, 512)
-    full = np.moveaxis(thirds(full.reshape(2, 384, 512)), 0, 1).reshape(2, 1152, 512)
+    full = np.moveaxis(thirds(full.reshape(2, 384, 512)), 0, 1)
+    full = [full[:, :, :128].reshape(2, 384, 512), full[:, :, 128:].reshape(2, 768, 512)]
+    full = np.concatenate(full, axis=1)
     return full[0], full[1]
 
 
@@ -360,30 +362,33 @@
             y_ref[to, pl.ds(256 + 128 * h, 128)] = i * cs - r * sn
 
     def row_products(s, r, base, pieces, ready):
-        def value(table, v):
-            total = None
-            for n, part in enumerate(split_n(v, pieces)):
-                out = mm(table[: 384 * (pieces - n)], part, ((1,), (1,)))
-                for k in range(pieces - n):
-                    one = out[384 * k : 384 * k + 384]
-                    total = one if total is None else total + one
-            return total
-
-        def product(step, _):
-            out = value(T["fg"], y_ref[pl.ds(pl.multiple_of(step * 256, 256), 256), :])
-            for g in range(2):
-                to = pl.ds(pl.multiple_of((2 * step + g) * 128, 128), 128)
-                for m in range(3):
-                    s[m, to, :] = out[128 * m : 128 * m + 128, 128 * g : 128 * g + 128]
-            return 0
-
-        lax.fori_loop(0, 4, product, 0)
-        tail = value(T["fs"], y_ref[:64, :])
-        for m in range(3):
-            s[m, :128, :64] = tail[128 * m : 128 * m + 128]
-        ready()
-        for m in range(3):
-            send(s, r, m, base + m, 8 if m < 2 else 6)
+        for start, size, ms in ((0, 128, (0,)), (384, 256, (1, 2))):
+
+            def value(table, v):
+                total = None
+                for n, part in enumerate(split_n(v, pieces)):
+                    out = mm(table[start : start + size * (pieces - n)], part, ((1,), (1,)))
+                    for k in range(pieces - n):
+                        one = out[size * k : size * k + size]
+                        total = one if total is None else total + one
+                return total
+
+            def product(step, _):
+                out = value(T["fg"], y_ref[pl.ds(pl.multiple_of(step * 256, 256), 256), :])
+                for g in range(2):
+                    to = pl.ds(pl.multiple_of((2 * step + g) * 128, 128), 128)
+                    for n, m in enumerate(ms):
+                        s[m, to, :] = out[128 * n : 128 * n + 128, 128 * g : 128 * g + 128]
+                return 0
+
+            lax.fori_loop(0, 4, product, 0)
+            tail = value(T["fs"], y_ref[:64, :])
+            for n, m in enumerate(ms):
+                s[m, :128, :64] = tail[128 * n : 128 * n + 128]
+            if start == 0:
+                ready()
+            for m in ms:
+                send(s, r, m, base + m, 8 if m < 2 else 6)
 
     load(-1).wait()
     load(0).wait()

time: 174 us -> 171 us (0.983)
  Pallas kernels: 168 us -> 164 us
    pallas_call x1, Pallas kernels: 168 us -> 164 us  [local(): pl.pallas_call(functools.partial(kernel, names), out_shape=[jax.ShapeDtyp...]
where the time goes in v5:
time: 171 us; the launch traced here: 170 us
  Pallas kernels  164 us (96%)
  local copies, waits for them, and re-layouts  5.4 us (3%)
    pallas_call x1, Pallas kernels, local(): pl.pallas_call(functools.partial(kernel, names), out_shape=[jax.ShapeDtyp...  164 us
    unnamed x7, local copies, waits for them, and re-layouts  5.4 us

profile of v5, /device:TPU:0, one launch (start us, length us, event | category | flops | bytes accessed | tf_op | source)
XLA Modules:
  0.0 170.5 jit_solution(12490540068689001855)
XLA Ops:
  0.6 164.4 %shard_map.220 = (f32[64,8192]{1,0:T(8,128)}, f32[128,4096]{1,0:T(8,128)}, f32[64,2048]{1,0:T(8,128)}) custom-call(f32[64,8192]{1,0:T(8,128)} %refs_0_.1, f32[2,16,256]{2,1,0:T(8,128)} %constant.40.clone.refs_1_, bf16[1152,512]{1,0:T(8,128)(2,1)} %constant.41.clone.refs_2_, bf16[1152,512]{1,0:T(8,128)(2,1)} %constant.42.clone.refs_3_, ...), custom_call_target="tpu_custom_call" | custom-call | tf_op jit(solution)/shard_map/pallas_call | solution.py:807
  165.0 0.0 copy-start
  165.1 3.2 %copy.27 = f32[64,8192]{1,0:T(8,128)} copy(f32[64,8192]{1,0:T(8,128)} %get-tuple-element.6) | data formatting | bytes 4194304
  168.3 0.0 copy-done
  168.3 0.0 copy-start.1
  168.3 1.3 copy.28
  169.6 0.1 copy-done.1
  169.7 0.8 copy.29
Async XLA Ops:
  165.0 3.2 %copy-start = (f32[128,4096]{1,0:T(8,128)S(1)}, f32[128,4096]{1,0:T(8,128)}, u32[]{:S(2)}) copy-start(f32[128,4096]{1,0:T(8,128)} %get-tuple-element.7) | copy-start | bytes 6291460
  168.3 1.4 copy-start.1
